TPU v7x, 32 devices: a whole 2x2x4 slice. The times are simulated.
32 devices in a mesh: grp: 2 (over y), gx: 16 (over z, x, core).
Axes of the slice: x: 2, y: 2, z: 4, core: 2. Of those that a mesh axis runs over, the one named last changes fastest.
Arguments:
- tokens: bfloat16 [64, 6144], P(('grp', 'gx')), parts along dimension 0, may hold values from -6 to 6
- weight_hidden: bfloat16 [6144, 32768], P(None, 'gx'), may hold values from -0.078125 to 0.078125
- bias_hidden: bfloat16 [32768], replicated, may hold values from -3 to 3
- weight_output: bfloat16 [6144, 32768], P(None, 'gx'), may hold values from -0.03125 to 0.03125
- bias_output: bfloat16 [6144], replicated, may hold values from -3 to 3
- cotangent: bfloat16 [64, 6144], P(('grp', 'gx')), parts along dimension 0, may hold values from -6 to 6
Outputs:
- layer_output: bfloat16 [64, 6144], P(('grp', 'gx')), parts along dimension 0
- grad_tokens: bfloat16 [64, 6144], P(('grp', 'gx')), parts along dimension 0
- grad_weight_hidden: bfloat16 [6144, 65536], P(None, ('grp', 'gx')), parts along dimension 1
- grad_bias_hidden: float32 [65536], P(('grp', 'gx')), parts along dimension 0
- grad_weight_output: bfloat16 [6144, 65536], P(None, ('grp', 'gx')), parts along dimension 1
- grad_bias_output: float32 [12288], P('grp'), parts along dimension 0
There are 2 independent parts, one for each index of `grp`. A program takes and returns all parts, laid end to end along the dimension named above; an argument that names none is the same for every part. Nothing has to cross between parts.
All inputs are finite; a program needn't handle non-finite values.
Results may differ from a plain program's by a relative error of at most 0.005.
Values may be sent and summed in bfloat16 or wider, within the bound.
No kernel may reach another device: no remote copies, remote signals or barrier semaphores. Data moves between devices by JAX's collectives and lax.ppermute only.
A program may use at most 192 MiB of HBM per device.

v0:
```python
import jax
import jax.numpy as jnp
from jax import lax
from jax.sharding import PartitionSpec as P


def gelu_tanh(value):
    return jax.nn.gelu(value, approximate=True)


def contract_rows(left, right):
    return lax.dot_general(
        left, right, (((0,), (0,)), ((), ())), preferred_element_type=jnp.float32
    )


def contract_last(left, right):
    return lax.dot_general(
        left, right, (((1,), (1,)), ((), ())), preferred_element_type=jnp.float32
    )


def shards(tokens, weight_hidden, bias_hidden, weight_output, bias_output, cotangent):
    devices = lax.axis_size("gx")
    position = lax.axis_index("gx")
    narrow = weight_hidden.shape[1]
    stacked = jnp.stack([tokens, cotangent])
    gathered = lax.all_gather(stacked, "gx", axis=1, tiled=True)
    bias_table = bias_hidden.reshape(devices, narrow).astype(jnp.float32)
    grad_bias_output = jnp.sum(gathered[1].astype(jnp.float32), axis=0)
    out_bias = bias_output.astype(jnp.float32)
    every_token = gathered[0]
    every_grad = gathered[1]
    own_bias = lax.dynamic_index_in_dim(bias_table, position, 0, keepdims=False)
    hidden = jnp.dot(every_token, weight_hidden, preferred_element_type=jnp.float32) + own_bias
    active = gelu_tanh(hidden).astype(jnp.bfloat16)
    block = active
    summed_output = lax.psum_scatter(
        contract_last(block, weight_output), "gx", scatter_dimension=0, tiled=True
    )
    grad_active = jnp.dot(every_grad, weight_output, preferred_element_type=jnp.float32)
    _, backward = jax.vjp(gelu_tanh, hidden)
    grad_hidden = backward(grad_active)[0].astype(jnp.bfloat16)
    grad_weight_output = contract_rows(every_grad, active)
    grad_weight_hidden = contract_rows(every_token, grad_hidden)
    grad_bias_hidden = jnp.sum(grad_hidden.astype(jnp.float32), axis=0)
    block = grad_hidden
    summed_grad = lax.psum_scatter(
        contract_last(block, weight_hidden), "gx", scatter_dimension=0, tiled=True
    )
    layer_output = (summed_output + out_bias).astype(jnp.bfloat16)
    grad_tokens = summed_grad.astype(jnp.bfloat16)
    return (
        layer_output,
        grad_tokens,
        grad_weight_hidden.astype(jnp.bfloat16),
        grad_bias_hidden,
        grad_weight_output.astype(jnp.bfloat16),
        grad_bias_output,
    )


def solution(mesh):
    in_specs = (
        P(("grp", "gx"), None),
        P(None, "gx"),
        P(),
        P(None, "gx"),
        P(),
        P(("grp", "gx"), None),
    )
    out_specs = (
        P(("grp", "gx"), None),
        P(("grp", "gx"), None),
        P(None, ("grp", "gx")),
        P(("grp", "gx")),
        P(None, ("grp", "gx")),
        P("grp"),
    )
    return jax.shard_map(shards, mesh=mesh, in_specs=in_specs, out_specs=out_specs, check_vma=False)
```

profile of v0, /device:TPU:0, one launch (start us, length us, event | category | flops | bytes accessed | tf_op | source)
XLA Modules:
  0.0 186.1 jit_solution(6476498850734445520)
XLA Ops:
  7.2 0.0 all-reduce.5.cloned.1.call-start
  7.2 0.8 pad_maximum_fusion
  8.1 0.9 reshape.16
  9.0 25.4 %all_gather.3 = bf16[2,32,6144]{2,0,1:T(2,128)(2,1)S(1)} all-gather(bf16[2,2,6144]{2,0,1:T(2,128)(2,1)S(1)} %copy.12), channel_id=1, replica_groups=mesh['grp'=2,'gx'=16] {'gx'}, dimensions={1}, use_global_device_ids=true | all-gather | bytes 835584 | tf_op jit(solution)/shard_map/all_gather | solution.py:28
  34.4 1.1 fusion.10
  35.5 10.4 %convolution_add_fusion = f32[32,2048]{1,0:T(8,128)S(1)} fusion(bf16[6144,2048]{1,0:T(8,128)(2,1)} %param.7, bf16[1,32,6144]{2,0,1:T(2,128)(2,1)S(1)} %get-tuple-element.7, f32[2048]{0:T(1024)S(1)} %bitcast.24), kind=kOutput, calls=%fused_computation.2 | convolution fusion | flops 805371904 | bytes 25829376 | tf_op jit(solution)/shard_map/dot_general | solution.py:35
  45.9 13.1 %fusion.8 = f32[32,6144]{1,0:T(8,128)} fusion(bf16[6144,2048]{1,0:T(8,128)(2,1)} %param.9, f32[32,2048]{1,0:T(8,128)S(1)} %convolution_add_fusion), kind=kOutput, calls=%fused_computation.22 | convolution fusion | flops 805896192 | bytes 26214400 | tf_op jit(solution)/shard_map/dot_general | solution.py:18
  59.0 0.0 all-reduce.5.cloned.1.call-update
  59.0 11.4 %convert_reduce_fusion.1 = (f32[2048]{0:T(1024)}, bf16[32,2048]{1,0:T(8,128)(2,1)S(1)}) fusion(f32[32,2048]{1,0:T(8,128)S(1)} %convolution_add_fusion, bf16[6144,2048]{1,0:T(8,128)(2,1)} %param.9, bf16[1,32,6144]{2,0,1:T(2,128)(2,1)S(1)} %get-tuple-element.6), kind=kOutput, calls=%fused_computation.15 | convolution fusion | flops 806746112 | bytes 25960448 | tf_op jit(solution)/shard_map/dot_general | solution.py:41
  70.4 12.4 %convolution_convert_fusion = bf16[6144,2048]{1,0:T(8,128)(2,1)} fusion(f32[32,2048]{1,0:T(8,128)S(1)} %convolution_add_fusion, bf16[1,32,6144]{2,0,1:T(2,128)(2,1)S(1)} %get-tuple-element.6), kind=kOutput, calls=%fused_computation | convolution fusion | flops 818479104 | bytes 25821184 | tf_op jit(solution)/shard_map/dot_general | solution.py:12
  82.8 12.3 %fusion.11 = f32[32,6144]{1,0:T(8,128)S(1)} fusion(bf16[32,2048]{1,0:T(8,128)(2,1)S(1)} %get-tuple-element.9, bf16[6144,2048]{1,0:T(8,128)(2,1)} %param.7), kind=kOutput, calls=%fused_computation.25 | convolution fusion | flops 805306368 | bytes 26083328 | tf_op jit(solution)/shard_map/dot_general | solution.py:18
  95.1 0.0 copy-start.1
  95.1 0.0 copy-start
  95.1 12.4 %convolution_convert_fusion.1 = bf16[6144,2048]{1,0:T(8,128)(2,1)} fusion(bf16[32,2048]{1,0:T(8,128)(2,1)S(1)} %get-tuple-element.9, bf16[1,32,6144]{2,0,1:T(2,128)(2,1)S(1)} %get-tuple-element.7), kind=kOutput, calls=%fused_computation.1 | convolution fusion | flops 817889280 | bytes 25690112 | tf_op jit(solution)/shard_map/dot_general | solution.py:12
  107.6 67.4 %all-reduce.6 = bf16[32,6144]{1,0:T(8,128)(2,1)S(1)} all-reduce(f32[32,6144]{1,0:T(8,128)S(1)} %fusion.11), channel_id=3, replica_groups=mesh['grp'=2,'gx'=16] {'gx'}, use_global_device_ids=true, to_apply=%region_1.2.clone | all-reduce | flops 196608 | bytes 1179648
  174.9 0.0 copy-done.1
  174.9 0.6 dynamic-slice
  176.2 0.6 dynamic-slice_convert_fusion
  176.8 0.0 copy-done
  176.8 0.9 convert_reduce_fusion
  177.7 0.0 all-reduce.5.cloned.1.call-done
  177.7 1.6 fusion.7
  (3 shorter events, 0.1 us)
Async XLA Ops:
  7.2 170.5 %all-reduce.5.cloned.1.call-start = ((), (), s32[]{:S(2)}) async-start(), calls=%async_computation | async-start | bytes 1572864
  95.1 79.8 %copy-start.1 = (u32[32]{0:T(128)S(1)}, u32[32]{0:T(128)}, u32[]{:S(2)}) copy-start(u32[32]{0:T(128)} %constant.28) | copy-start | bytes 388
  95.1 81.7 %copy-start = (bf16[6144]{0:T(1024)(128)(2,1)S(1)}, bf16[6144]{0:T(1024)(128)(2,1)}, u32[]{:S(2)}) copy-start(bf16[6144]{0:T(1024)(128)(2,1)} %param.10) | copy-start | bytes 36868
Sparse Core Ops, SparseCore 0:
  59.1 89.3 all-reduce.4
where the time goes:
time: 186 us
  blocking collectives  92.8 us (50%)
  matrix products  72 us (39%)
  between operations  14.8 us (8%)
  local copies, waits for them, and re-layouts  3.26 us (2%)
  other arithmetic  3.25 us (2%)
    unnamed x1, blocking collectives  67.4 us
    all_gather x1, blocking collectives, shards(): gathered = lax.all_gather(stacked, 'gx', axis=1, tiled=True)  25.4 us
    dot_general x2, matrix products, contract_last(): lax.dot_general(left, right, (((1,), (1,)), ((), ())), preferred_element_...  25.4 us
    dot_general x2, matrix products, contract_rows(): lax.dot_general(left, right, (((0,), (0,)), ((), ())), preferred_element_...  24.8 us
    dot_general x1, matrix products, shards(): jnp.dot(every_grad, weight_output, preferred_element_type=jnp.float32)  11.4 us
    dot_general x1, matrix products, shards(): jnp.dot(every_token, weight_hidden, preferred_element_type=jnp.float32)  10.4 us
  transfers between devices with their start and end apart: 1, of which 0 were waited for; matrix products, arithmetic and copies ran while one was open for 27% of the time, Pallas kernels for 0%

commit v1 on v0

v1 whole, which is shorter than its diff:
```python
import functools
import math

import jax
import jax.numpy as jnp
from jax import lax
from jax.experimental import pallas as pl
from jax.experimental.pallas import tpu as pltpu
from jax.sharding import PartitionSpec as P

F32 = jnp.float32
BF16 = jnp.bfloat16
SCALE = math.sqrt(2.0 / math.pi)
CUBE = 0.044715
VMEM = 56 * 2**20


def product(left, right, dims):
    return lax.dot_general(left, right, (dims, ((), ())), preferred_element_type=F32)


def gelu_and_slope(value):
    square = value * value
    bent = jnp.tanh(SCALE * (value + CUBE * value * square))
    half = 0.5 * (1.0 + bent)
    slope = half + 0.5 * value * (1.0 - bent * bent) * (SCALE * (1.0 + 3.0 * CUBE * square))
    return value * half, slope


def weights_body(both, bias, weight_hidden, weight_output, active, grad_hidden, grad_bias_hidden,
                 grad_bias_output, partial):
    tokens = both[0]
    cotangent = both[1]

    @pl.when(pl.program_id(0) == 0)
    def _():
        partial[...] = jnp.zeros_like(partial)
        grad_bias_output[...] = jnp.sum(cotangent.astype(F32), axis=0, keepdims=True)

    hidden = product(tokens, weight_hidden[...], ((1,), (0,))) + bias[...].astype(F32)
    value, slope = gelu_and_slope(hidden)
    value = value.astype(BF16)
    active[...] = value
    grad = (product(cotangent, weight_output[...], ((1,), (0,))) * slope).astype(BF16)
    grad_hidden[...] = grad
    grad_bias_hidden[...] = jnp.sum(grad.astype(F32), axis=0, keepdims=True)
    partial[0] += product(value, weight_output[...], ((1,), (1,)))
    partial[1] += product(grad, weight_hidden[...], ((1,), (1,)))


def weights_pass(both, bias, weight_hidden, weight_output):
    _, count, width = both.shape
    units = weight_hidden.shape[1]
    tile = min(256, units)
    whole = lambda i: (0, 0)
    across = lambda i: (0, i)
    return pl.pallas_call(
        weights_body,
        grid=(units // tile,),
        in_specs=[
            pl.BlockSpec((2, count, width), lambda i: (0, 0, 0)),
            pl.BlockSpec((1, tile), across),
            pl.BlockSpec((width, tile), across),
            pl.BlockSpec((width, tile), across),
        ],
        out_specs=[
            pl.BlockSpec((count, tile), across),
            pl.BlockSpec((count, tile), across),
            pl.BlockSpec((1, tile), across),
            pl.BlockSpec((1, width), whole),
            pl.BlockSpec((2, count, width), lambda i: (0, 0, 0)),
        ],
        out_shape=[
            jax.ShapeDtypeStruct((count, units), BF16),
            jax.ShapeDtypeStruct((count, units), BF16),
            jax.ShapeDtypeStruct((1, units), F32),
            jax.ShapeDtypeStruct((1, width), F32),
            jax.ShapeDtypeStruct((2, count, width), F32),
        ],
        compiler_params=pltpu.CompilerParams(vmem_limit_bytes=VMEM),
        cost_estimate=pl.CostEstimate(
            flops=8 * count * width * units, bytes_accessed=4 * width * units, transcendentals=count * units
        ),
        name="weights_pass",
    )(both, bias, weight_hidden, weight_output)


def outer_body(left, right, result):
    result[...] = product(left[0], right[...], ((0,), (0,))).astype(BF16)


def outer(both, which, right, name):
    _, count, width = both.shape
    units = right.shape[1]
    tile = min(512, width)
    return pl.pallas_call(
        outer_body,
        grid=(width // tile,),
        in_specs=[
            pl.BlockSpec((1, count, tile), lambda i: (which, 0, i)),
            pl.BlockSpec((count, units), lambda i: (0, 0)),
        ],
        out_specs=pl.BlockSpec((tile, units), lambda i: (i, 0)),
        out_shape=jax.ShapeDtypeStruct((width, units), BF16),
        compiler_params=pltpu.CompilerParams(vmem_limit_bytes=VMEM),
        cost_estimate=pl.CostEstimate(
            flops=2 * count * width * units, bytes_accessed=2 * width * units, transcendentals=0
        ),
        name=name,
    )(both, right)


def levels_of(devices):
    levels = [(1, 2)] if devices > 1 else []
    unit = 2
    if (devices.bit_length() - 1) % 2 == 0 and devices > 2:
        levels.append((unit, 2))
        unit *= 2
    while unit < devices:
        levels.append((unit, 4))
        unit *= 4
    return levels


def shards(tokens, weight_hidden, bias_hidden, weight_output, bias_output, cotangent):
    devices = lax.axis_size("gx")
    position = lax.axis_index("gx")
    narrow = weight_hidden.shape[1]
    width = tokens.shape[1]
    levels = levels_of(devices)

    def swap(value, step):
        return lax.ppermute(value, "gx", [(i, i ^ step) for i in range(devices)])

    both = jnp.stack([tokens, cotangent])
    for unit, size in reversed(levels):
        both = jnp.concatenate([both] + [swap(both, unit * j) for j in range(1, size)], axis=1)
    bias = lax.dynamic_slice(bias_hidden, (position * narrow,), (narrow,))
    active, grad_hidden, grad_bias_hidden, grad_bias_output, partial = weights_pass(
        both, bias.reshape(1, narrow), weight_hidden, weight_output
    )

    for unit, size in levels:
        pieces = partial.reshape(2, size, -1, width)
        kind = F32 if unit == 1 else BF16
        arrived = [swap(pieces[:, j].astype(kind), unit * j) for j in range(1, size)]
        partial = pieces[:, 0]
        for piece in arrived:
            partial = partial + piece.astype(F32)

    grad_weight_output = outer(both, 1, active, "outer_output")
    grad_weight_hidden = outer(both, 0, grad_hidden, "outer_hidden")
    layer_output = (partial[0] + bias_output.astype(F32)).astype(BF16)
    grad_tokens = partial[1].astype(BF16)
    return (
        layer_output,
        grad_tokens,
        grad_weight_hidden,
        grad_bias_hidden.reshape(narrow),
        grad_weight_output,
        grad_bias_output.reshape(width),
    )


def solution(mesh):
    in_specs = (
        P(("grp", "gx"), None),
        P(None, "gx"),
        P(),
        P(None, "gx"),
        P(),
        P(("grp", "gx"), None),
    )
    out_specs = (
        P(("grp", "gx"), None),
        P(("grp", "gx"), None),
        P(None, ("grp", "gx")),
        P(("grp", "gx")),
        P(None, ("grp", "gx")),
        P("grp"),
    )
    return jax.shard_map(shards, mesh=mesh, in_specs=in_specs, out_specs=out_specs, check_vma=False)
```

time: 186 us -> 95.9 us (0.52)
  blocking collectives: 92.8 us -> 0 us
  matrix products: 72 us -> 0 us
  Pallas kernels: 0 us -> 58.4 us
  between operations: 14.8 us -> 0.76 us
  starting transfers between devices: 0.04 us -> 12.7 us
  waiting for transfers between devices: 0.02 us -> 11.2 us
  local copies, waits for them, and re-layouts: 3.26 us -> 7.51 us
    dot_general x6 -> x0, matrix products: 72 us -> none  [the longest x2 25.4 us: contract_last(): lax.dot_general(left, right, (((1,), (1,)), ((), ())), preferred_element_...]
    unnamed x1 -> x0, blocking collectives: 67.4 us -> none
    pallas_call x0 -> x3, Pallas kernels: none -> 58.4 us  [the longest x1 30.4 us: weights_pass(): pl.pallas_call(weights_body, grid=(units // tile,), in_specs=[pl.BlockSpe...]
    all_gather x1 -> x0, blocking collectives: 25.4 us -> none  [shards(): gathered = lax.all_gather(stacked, 'gx', axis=1, tiled=True)]
    ppermute x0 -> x10, starting transfers between devices: none -> 12.7 us  [swap(): return lax.ppermute(value, 'gx', [(i, i ^ step) for i in range(devices)])]
    ppermute x0 -> x10, waiting for transfers between devices: none -> 11.2 us  [swap(): return lax.ppermute(value, 'gx', [(i, i ^ step) for i in range(devices)])]
    concatenate x0 -> x2, local copies, waits for them, and re-layouts: none -> 3.44 us  [shards(): jnp.concatenate([both] + [swap(both, unit * j) for j in range(1, size)],...]
  transfers between devices with their start and end apart: 1 -> 10, of which waited for: 0 -> 5; matrix products, arithmetic and copies ran while one was open for 27% -> 1% of each run, Pallas kernels for 0% -> 30%
where the time goes in v1:
time: 95.9 us; the launch traced here: 94.6 us
  Pallas kernels  58.4 us (61%)
  starting transfers between devices  12.7 us (13%)
  waiting for transfers between devices  11.2 us (12%)
  local copies, waits for them, and re-layouts  7.51 us (8%)
  other arithmetic  4.11 us (4%)
    pallas_call x1, Pallas kernels, weights_pass(): pl.pallas_call(weights_body, grid=(units // tile,), in_specs=[pl.BlockSpe...  30.4 us
    pallas_call x2, Pallas kernels, outer(): pl.pallas_call(outer_body, grid=(width // tile,), in_specs=[pl.BlockSpec(...  28 us
    ppermute x10, starting transfers between devices, swap(): return lax.ppermute(value, 'gx', [(i, i ^ step) for i in range(devices)])  12.7 us
    ppermute x10, waiting for transfers between devices, swap(): return lax.ppermute(value, 'gx', [(i, i ^ step) for i in range(devices)])  11.2 us
    concatenate x2, local copies, waits for them, and re-layouts, shards(): jnp.concatenate([both] + [swap(both, unit * j) for j in range(1, size)],...  3.44 us
  transfers between devices with their start and end apart: 10, of which 5 were waited for; matrix products, arithmetic and copies ran while one was open for 1% of the time, Pallas kernels for 30%

profile of v1, /device:TPU:0, one launch (start us, length us, event | category | flops | bytes accessed | tf_op | source)
XLA Modules:
  0.0 94.6 jit_solution(10937437478621735802)
XLA Ops:
  0.6 0.8 pad_maximum_fusion.1
  1.5 5.1 %collective-permute-start.2 = (bf16[2,2,6144]{2,1,0:T(2,128)(2,1)S(1)}, bf16[2,2,6144]{2,1,0:T(2,128)(2,1)S(1)}, u32[]{:S(2)}, u32[]{:S(2)}) collective-permute-start(bf16[2,2,6144]{2,1,0:T(2,128)(2,1)S(1)} %pad_maximum_fusion.1), channel_id=1, source_target_pairs={{0,12},{1,13},{2,14},{3,15},{4,8},{5,9},{6,10},{7,11},{8,4},{9,5},... | collective-permute-start | bytes 147464 | tf_op jit(solution)/shard_map/ppermute | solution.py:133
  6.6 0.6 collective-permute-start
  7.2 1.6 %collective-permute-done.2 = bf16[2,2,6144]{2,1,0:T(2,128)(2,1)S(1)} collective-permute-done((bf16[2,2,6144]{2,1,0:T(2,128)(2,1)S(1)}, bf16[2,2,6144]{2,1,0:T(2,128)(2,1)S(1)}, u32[]{:S(2)}, u32[]{:S(2)}) %collective-permute-start.2) | collective-permute-done | bytes 49184 | tf_op jit(solution)/shard_map/ppermute | solution.py:133
  8.8 2.8 %collective-permute-done.1 = bf16[2,2,6144]{2,1,0:T(2,128)(2,1)S(1)} collective-permute-done((bf16[2,2,6144]{2,1,0:T(2,128)(2,1)S(1)}, bf16[2,2,6144]{2,1,0:T(2,128)(2,1)S(1)}, u32[]{:S(2)}, u32[]{:S(2)}) %collective-permute-start.1) | collective-permute-done | bytes 49184 | tf_op jit(solution)/shard_map/ppermute | solution.py:133
  11.6 1.0 %pad_maximum_fusion = bf16[2,8,6144]{2,1,0:T(8,128)(2,1)S(1)} fusion(bf16[2,2,6144]{2,1,0:T(2,128)(2,1)S(1)} %collective-permute-done.2, bf16[2,2,6144]{2,1,0:T(2,128)(2,1)S(1)} %collective-permute-done.1, bf16[2,2,6144]{2,1,0:T(2,128)(2,1)S(1)} %collective-permute-done, bf16[1,2,6144]{2,1,0:T(2,128)(2,1)} %bitcast.49, bf16[1,2,6144]{2,1,0:T(2,128)(2,1)} %bitcast.51), kind=kLoop, calls=%fused_computation.7 | loop fusion | flops 983040 | bytes 393216 | tf_op jit(solution)/shard_map/concatenate | solution.py:137
  12.6 1.6 %collective-permute-start.3 = (bf16[2,8,6144]{2,1,0:T(8,128)(2,1)S(1)}, bf16[2,8,6144]{2,1,0:T(8,128)(2,1)S(1)}, u32[]{:S(2)}, u32[]{:S(2)}) collective-permute-start(bf16[2,8,6144]{2,1,0:T(8,128)(2,1)S(1)} %pad_maximum_fusion), channel_id=1, source_target_pairs={{0,2},{1,3},{2,0},{3,1},{4,6},{5,7},{6,4},{7,5},{8,10},{9,11},{10,... | collective-permute-start | bytes 589832 | tf_op jit(solution)/shard_map/ppermute | solution.py:133
  14.1 4.3 %collective-permute-done.3 = bf16[2,8,6144]{2,1,0:T(8,128)(2,1)S(1)} collective-permute-done((bf16[2,8,6144]{2,1,0:T(8,128)(2,1)S(1)}, bf16[2,8,6144]{2,1,0:T(8,128)(2,1)S(1)}, u32[]{:S(2)}, u32[]{:S(2)}) %collective-permute-start.3) | collective-permute-done | bytes 196640 | tf_op jit(solution)/shard_map/ppermute | solution.py:133
  18.4 0.4 concatenate.12
  18.9 0.7 dynamic_slice.3
  19.6 0.6 reshape.36.bias
  20.6 3.0 %concatenate.13.both.left = bf16[2,32,6144]{2,1,0:T(8,128)(2,1)} concatenate(bf16[2,2,6144]{2,1,0:T(2,128)(2,1)S(1)} %pad_maximum_fusion.1, bf16[2,2,6144]{2,1,0:T(2,128)(2,1)S(1)} %collective-permute-done, bf16[2,2,6144]{2,1,0:T(2,128)(2,1)S(1)} %collective-permute-done.1, bf16[2,2,6144]{2,1,0:T(2,128)(2,1)S(1)} %collective-permute-done.2, ...), dimensions={1} | concatenate | bytes 1572864 | tf_op jit(solution)/shard_map/concatenate | solution.py:137
  23.6 30.4 %weights_pass.1 = (bf16[32,2048]{1,0:T(8,128)(2,1)}, bf16[32,2048]{1,0:T(8,128)(2,1)}, f32[1,2048]{1,0:T(1,128)}, f32[1,6144]{1,0:T(1,128)}, f32[2,32,6144]{2,1,0:T(8,128)}) custom-call(bf16[2,32,6144]{2,1,0:T(8,128)(2,1)} %concatenate.13.both.left, bf16[1,2048]{1,0:T(2,128)(2,1)} %reshape.36.bias, bf16[6144,2048]{1,0:T(8,128)(2,1)} %weight_hidden.1, ...), custom_call_target="tpu_custom_call" | custom-call | flops 3221225472 | bytes 50331648 | tf_op jit(solution)/shard_map/weights_pass/pallas_call | solution.py:57
  54.0 1.2 %slice_bitcast_fusion = f32[2,16,6144]{2,1,0:T(8,128)S(1)} fusion(f32[2,2,16,6144]{3,2,1,0:T(8,128)} %bitcast.46), kind=kLoop, calls=%fused_computation | loop fusion | bytes 1572864 | tf_op jit(solution)/shard_map/squeeze | solution.py:146
  55.4 2.2 %collective-permute-done.5 = f32[2,16,6144]{2,1,0:T(8,128)S(1)} collective-permute-done((f32[2,16,6144]{2,1,0:T(8,128)S(1)}, f32[2,16,6144]{2,1,0:T(8,128)S(1)}, u32[]{:S(2)}, u32[]{:S(2)}) %collective-permute-start.5) | collective-permute-done | bytes 786464 | tf_op jit(solution)/shard_map/ppermute | solution.py:133
  57.6 1.2 %fusion = f32[2,16,6144]{2,1,0:T(8,128)S(1)} fusion(f32[2,16,6144]{2,1,0:T(8,128)S(1)} %collective-permute-done.5, f32[2,2,16,6144]{3,2,1,0:T(8,128)} %bitcast.47), kind=kLoop, calls=%fused_computation.2 | loop fusion | flops 196608 | bytes 2359296 | tf_op jit(solution)/shard_map/add | solution.py:149
  58.8 0.6 copy.17
  59.5 1.6 %collective-permute-start.6 = (bf16[2,8,6144]{2,0,1:T(2,128)(2,1)S(1)}, bf16[2,8,6144]{2,0,1:T(2,128)(2,1)S(1)}, u32[]{:S(2)}, u32[]{:S(2)}) collective-permute-start(bf16[2,8,6144]{2,0,1:T(2,128)(2,1)S(1)} %fusion.2), channel_id=1, source_target_pairs={{0,2},{1,3},{2,0},{3,1},{4,6},{5,7},{6,4},{7,5},{8,10},{9,11},{10,... | collective-permute-start | bytes 589832 | tf_op jit(solution)/shard_map/ppermute | solution.py:133
  61.1 14.0 %outer_hidden.1 = bf16[6144,2048]{1,0:T(8,128)(2,1)} custom-call(bf16[2,32,6144]{2,1,0:T(8,128)(2,1)} %concatenate.13.both.left, bf16[32,2048]{1,0:T(8,128)(2,1)} %get-tuple-element.12.right), custom_call_target="tpu_custom_call" | custom-call | flops 805306368 | bytes 25165824 | tf_op jit(solution)/shard_map/outer_hidden/pallas_call | solution.py:96
  75.6 0.8 collective-permute-start.7
  76.4 2.7 %collective-permute-start.9 = (bf16[2,2,6144]{2,0,1:T(2,128)(2,1)S(1)}, bf16[2,2,6144]{2,0,1:T(2,128)(2,1)S(1)}, u32[]{:S(2)}, u32[]{:S(2)}) collective-permute-start(bf16[2,2,6144]{2,0,1:T(2,128)(2,1)S(1)} %get-tuple-element.17), channel_id=1, source_target_pairs={{0,12},{1,13},{2,14},{3,15},{4,8},{5,9},{6,10},{7,11},{8,4},{9,5},... | collective-permute-start | bytes 147464 | tf_op jit(solution)/shard_map/ppermute | solution.py:133
  79.2 14.0 %outer_output.1 = bf16[6144,2048]{1,0:T(8,128)(2,1)} custom-call(bf16[2,32,6144]{2,1,0:T(8,128)(2,1)} %concatenate.13.both.left, bf16[32,2048]{1,0:T(8,128)(2,1)} %get-tuple-element.14.right), custom_call_target="tpu_custom_call" | custom-call | flops 805306368 | bytes 25165824 | tf_op jit(solution)/shard_map/outer_output/pallas_call | solution.py:96
  93.4 0.6 copy.23
  94.0 0.6 fusion.6
  (20 shorter events, 1.5 us)
Async XLA Ops:
  1.5 7.3 %collective-permute-start.2 = (bf16[2,2,6144]{2,1,0:T(2,128)(2,1)S(1)}, bf16[2,2,6144]{2,1,0:T(2,128)(2,1)S(1)}, u32[]{:S(2)}, u32[]{:S(2)}) collective-permute-start(bf16[2,2,6144]{2,1,0:T(2,128)(2,1)S(1)} %pad_maximum_fusion.1), channel_id=1, source_target_pairs={{0,12},{1,13},{2,14},{3,15},{4,8},{5,9},{6,10},{7,11},{8,4},{9,5},... | collective-permute-start | bytes 147464 | tf_op jit(solution)/shard_map/ppermute | solution.py:133
  6.6 5.0 %collective-permute-start.1 = (bf16[2,2,6144]{2,1,0:T(2,128)(2,1)S(1)}, bf16[2,2,6144]{2,1,0:T(2,128)(2,1)S(1)}, u32[]{:S(2)}, u32[]{:S(2)}) collective-permute-start(bf16[2,2,6144]{2,1,0:T(2,128)(2,1)S(1)} %pad_maximum_fusion.1), channel_id=1, source_target_pairs={{0,8},{1,9},{2,10},{3,11},{4,12},{5,13},{6,14},{7,15},{8,0},{9,1},... | collective-permute-start | bytes 147464 | tf_op jit(solution)/shard_map/ppermute | solution.py:133
  6.6 5.0 %collective-permute-start = (bf16[2,2,6144]{2,1,0:T(2,128)(2,1)S(1)}, bf16[2,2,6144]{2,1,0:T(2,128)(2,1)S(1)}, u32[]{:S(2)}, u32[]{:S(2)}) collective-permute-start(bf16[2,2,6144]{2,1,0:T(2,128)(2,1)S(1)} %pad_maximum_fusion.1), channel_id=1, source_target_pairs={{0,4},{1,5},{2,6},{3,7},{4,0},{5,1},{6,2},{7,3},{8,12},{9,13},{10,... | collective-permute-start | bytes 147464 | tf_op jit(solution)/shard_map/ppermute | solution.py:133
  12.6 5.8 %collective-permute-start.3 = (bf16[2,8,6144]{2,1,0:T(8,128)(2,1)S(1)}, bf16[2,8,6144]{2,1,0:T(8,128)(2,1)S(1)}, u32[]{:S(2)}, u32[]{:S(2)}) collective-permute-start(bf16[2,8,6144]{2,1,0:T(8,128)(2,1)S(1)} %pad_maximum_fusion), channel_id=1, source_target_pairs={{0,2},{1,3},{2,0},{3,1},{4,6},{5,7},{6,4},{7,5},{8,10},{9,11},{10,... | collective-permute-start | bytes 589832 | tf_op jit(solution)/shard_map/ppermute | solution.py:133
  18.8 1.8 %collective-permute-start.4 = (bf16[2,16,6144]{2,1,0:T(8,128)(2,1)S(1)}, bf16[2,16,6144]{2,1,0:T(8,128)(2,1)S(1)}, u32[]{:S(2)}, u32[]{:S(2)}) collective-permute-start(bf16[2,16,6144]{2,1,0:T(8,128)(2,1)S(1)} %concatenate.12), channel_id=1, source_target_pairs={{0,1},{1,0},{2,3},{3,2},{4,5},{5,4},{6,7},{7,6},{8,9},{9,8},{10,11... | collective-permute-start | bytes 1179656 | tf_op jit(solution)/shard_map/ppermute | solution.py:133
  23.6 37.5 %copy-start = (bf16[6144]{0:T(1024)(128)(2,1)S(1)}, bf16[6144]{0:T(1024)(128)(2,1)}, u32[]{:S(2)}) copy-start(bf16[6144]{0:T(1024)(128)(2,1)} %param.10) | copy-start | bytes 36868
  55.2 2.4 %collective-permute-start.5 = (f32[2,16,6144]{2,1,0:T(8,128)S(1)}, f32[2,16,6144]{2,1,0:T(8,128)S(1)}, u32[]{:S(2)}, u32[]{:S(2)}) collective-permute-start(f32[2,16,6144]{2,1,0:T(8,128)S(1)} %slice_bitcast_fusion), channel_id=1, source_target_pairs={{0,1},{1,0},{2,3},{3,2},{4,5},{5,4},{6,7},{7,6},{8,9},{9,8},{10,11... | collective-permute-start | bytes 2359304 | tf_op jit(solution)/shard_map/ppermute | solution.py:133
  59.5 15.6 %collective-permute-start.6 = (bf16[2,8,6144]{2,0,1:T(2,128)(2,1)S(1)}, bf16[2,8,6144]{2,0,1:T(2,128)(2,1)S(1)}, u32[]{:S(2)}, u32[]{:S(2)}) collective-permute-start(bf16[2,8,6144]{2,0,1:T(2,128)(2,1)S(1)} %fusion.2), channel_id=1, source_target_pairs={{0,2},{1,3},{2,0},{3,1},{4,6},{5,7},{6,4},{7,5},{8,10},{9,11},{10,... | collective-permute-start | bytes 589832 | tf_op jit(solution)/shard_map/ppermute | solution.py:133
  75.6 17.5 %collective-permute-start.7 = (bf16[2,2,6144]{2,0,1:T(2,128)(2,1)S(1)}, bf16[2,2,6144]{2,0,1:T(2,128)(2,1)S(1)}, u32[]{:S(2)}, u32[]{:S(2)}) collective-permute-start(bf16[2,2,6144]{2,0,1:T(2,128)(2,1)S(1)} %get-tuple-element.16), channel_id=1, source_target_pairs={{0,4},{1,5},{2,6},{3,7},{4,0},{5,1},{6,2},{7,3},{8,12},{9,13},{10,... | collective-permute-start | bytes 147464 | tf_op jit(solution)/shard_map/ppermute | solution.py:133
  76.4 16.8 %collective-permute-start.9 = (bf16[2,2,6144]{2,0,1:T(2,128)(2,1)S(1)}, bf16[2,2,6144]{2,0,1:T(2,128)(2,1)S(1)}, u32[]{:S(2)}, u32[]{:S(2)}) collective-permute-start(bf16[2,2,6144]{2,0,1:T(2,128)(2,1)S(1)} %get-tuple-element.17), channel_id=1, source_target_pairs={{0,12},{1,13},{2,14},{3,15},{4,8},{5,9},{6,10},{7,11},{8,4},{9,5},... | collective-permute-start | bytes 147464 | tf_op jit(solution)/shard_map/ppermute | solution.py:133
  79.1 14.1 %collective-permute-start.8 = (bf16[2,2,6144]{2,0,1:T(2,128)(2,1)S(1)}, bf16[2,2,6144]{2,0,1:T(2,128)(2,1)S(1)}, u32[]{:S(2)}, u32[]{:S(2)}) collective-permute-start(bf16[2,2,6144]{2,0,1:T(2,128)(2,1)S(1)} %get-tuple-element.18), channel_id=1, source_target_pairs={{0,8},{1,9},{2,10},{3,11},{4,12},{5,13},{6,14},{7,15},{8,0},{9,1},... | collective-permute-start | bytes 147464 | tf_op jit(solution)/shard_map/ppermute | solution.py:133

commit v2 on v1

v2 whole, which is shorter than its diff:
```python
import functools
import math

import jax
import jax.numpy as jnp
from jax import lax
from jax.experimental import pallas as pl
from jax.experimental.pallas import tpu as pltpu
from jax.sharding import PartitionSpec as P

F32 = jnp.float32
BF16 = jnp.bfloat16
SCALE = math.sqrt(2.0 / math.pi)
CUBE = 0.044715
VMEM = 34 * 2**20
STEPS = 12
PASS = 4
HOP = 3
HELD = pl.BlockSpec(memory_space=pltpu.VMEM)


def held(value):
    return pltpu.with_memory_space_constraint(value, pltpu.VMEM)


def product(left, right, dims):
    return lax.dot_general(left, right, (dims, ((), ())), preferred_element_type=F32)


def gelu_and_slope(value):
    square = value * value
    bent = jnp.tanh(SCALE * (value + CUBE * value * square))
    half = 0.5 * (1.0 + bent)
    slope = half + 0.5 * value * (1.0 - bent * bent) * (SCALE * (1.0 + 3.0 * CUBE * square))
    return value * half, slope


def weights_body(mine, theirs, bias, weight_hidden, weight_output, active, grad_hidden, grad_bias_hidden,
                 grad_bias_output, both, keep, send, grad_weight_hidden, grad_weight_output, turned):
    near = mine.shape[1]
    rows, tile = grad_weight_output.shape

    @pl.when(pl.program_id(0) == 0)
    def _():
        both[:, :near] = mine[...]
        both[:, near:] = theirs[...]
        keep[...] = jnp.zeros_like(keep)
        send[...] = jnp.zeros_like(send)
        grad_bias_output[...] = jnp.sum(both[1].astype(F32), axis=0, keepdims=True)
        turned[0] = both[0, :, :rows].T
        turned[1] = both[1, :, :rows].T

    hidden = product(both[0], weight_hidden[...], ((1,), (0,))) + bias[...].astype(F32)
    value, slope = gelu_and_slope(hidden)
    value = value.astype(BF16)
    at = pl.program_id(0) * tile
    place = pl.ds(pl.multiple_of(at, tile), tile)
    active[:, place] = value
    grad = (product(both[1], weight_output[...], ((1,), (0,))) * slope).astype(BF16)
    grad_hidden[:, place] = grad
    grad_bias_hidden[...] = jnp.sum(grad.astype(F32), axis=0, keepdims=True)
    share = product(value, weight_output[...], ((1,), (1,)))
    keep[0] += share[:near]
    send[0] += share[near:]
    share = product(grad, weight_hidden[...], ((1,), (1,)))
    keep[1] += share[:near]
    send[1] += share[near:]
    grad_weight_hidden[...] = product(turned[0], grad, ((1,), (0,))).astype(BF16)
    grad_weight_output[...] = product(turned[1], value, ((1,), (0,))).astype(BF16)


def weights_pass(mine, theirs, bias, weight_hidden, weight_output, rows):
    _, near, width = mine.shape
    count = 2 * near
    units = weight_hidden.shape[1]
    tile = min(256 if count <= 64 else 128, units)
    across = lambda i: (0, i)
    return pl.pallas_call(
        weights_body,
        grid=(units // tile,),
        in_specs=[
            HELD,
            HELD,
            pl.BlockSpec((1, tile), across),
            pl.BlockSpec((width, tile), across),
            pl.BlockSpec((width, tile), across),
        ],
        out_specs=[
            HELD,
            HELD,
            pl.BlockSpec((1, tile), across),
            pl.BlockSpec((1, width), lambda i: (0, 0)),
            HELD,
            HELD,
            HELD,
            pl.BlockSpec((rows, tile), across),
            pl.BlockSpec((rows, tile), across),
        ],
        out_shape=[
            pltpu.VMEM((count, units), BF16),
            pltpu.VMEM((count, units), BF16),
            jax.ShapeDtypeStruct((1, units), F32),
            jax.ShapeDtypeStruct((1, width), F32),
            pltpu.VMEM((2, count, width), BF16),
            pltpu.VMEM((2, near, width), F32),
            pltpu.VMEM((2, near, width), F32),
            jax.ShapeDtypeStruct((width, units), BF16),
            jax.ShapeDtypeStruct((width, units), BF16),
        ],
        scratch_shapes=[pltpu.VMEM((2, rows, count), BF16)],
        compiler_params=pltpu.CompilerParams(vmem_limit_bytes=VMEM),
        cost_estimate=pl.CostEstimate(
            flops=12 * count * width * units, bytes_accessed=6 * width * units, transcendentals=count * units
        ),
        name="weights_pass",
    )(held(mine), held(theirs), bias, weight_hidden, weight_output)


def outer_body(first, both, active, grad_hidden, _hidden, _output, grad_weight_hidden, grad_weight_output):
    tile = grad_weight_output.shape[0]
    at = (first + pl.program_id(0)) * tile
    place = pl.ds(pl.multiple_of(at, tile), tile)
    grad_weight_hidden[...] = product(both[0, :, place], grad_hidden[...], ((0,), (0,))).astype(BF16)
    grad_weight_output[...] = product(both[1, :, place], active[...], ((0,), (0,))).astype(BF16)


def outer_rows(both, active, grad_hidden, grad_weight_hidden, grad_weight_output, first, steps, tile):
    _, count, width = both.shape
    units = active.shape[1]
    place = pl.BlockSpec((tile, units), lambda i: (first + i, 0))
    return pl.pallas_call(
        functools.partial(outer_body, first),
        grid=(steps,),
        in_specs=[
            HELD,
            HELD,
            HELD,
            pl.BlockSpec(memory_space=pl.ANY),
            pl.BlockSpec(memory_space=pl.ANY),
        ],
        out_specs=[place, place],
        out_shape=[jax.ShapeDtypeStruct((width, units), BF16)] * 2,
        input_output_aliases={3: 0, 4: 1},
        compiler_params=pltpu.CompilerParams(vmem_limit_bytes=VMEM),
        cost_estimate=pl.CostEstimate(
            flops=4 * count * steps * tile * units, bytes_accessed=4 * steps * tile * units, transcendentals=0
        ),
        name="outer_rows",
    )(held(both), held(active), held(grad_hidden), grad_weight_hidden, grad_weight_output)


def split_body(size, _after, *refs):
    parts, results = refs[:-size], refs[-size:]
    total = parts[0][...]
    for part in parts[1:]:
        total = total + part[...].astype(F32)
    rows = total.shape[1] // size
    for j, result in enumerate(results):
        result[...] = total[:, j * rows : (j + 1) * rows].astype(result.dtype)


def add_and_split(after, parts, size):
    _, rows, width = parts[0].shape
    cut = (2, rows // size, width)
    return pl.pallas_call(
        functools.partial(split_body, size),
        in_specs=[pl.BlockSpec(memory_space=pl.ANY)] + [HELD] * len(parts),
        out_specs=[HELD] * size,
        out_shape=[pltpu.VMEM(cut, F32)] + [pltpu.VMEM(cut, BF16)] * (size - 1),
        compiler_params=pltpu.CompilerParams(vmem_limit_bytes=VMEM),
        name="add_and_split",
    )(after, *[held(part) for part in parts])


def last_body(bias, *refs):
    parts, (layer_output, grad_tokens) = refs[:-2], refs[-2:]
    total = parts[0][...]
    for part in parts[1:]:
        total = total + part[...].astype(F32)
    layer_output[...] = (total[0] + bias[...].astype(F32)).astype(BF16)
    grad_tokens[...] = total[1].astype(BF16)


def last_sum(bias, parts):
    _, rows, width = parts[0].shape
    return pl.pallas_call(
        last_body,
        in_specs=[HELD] * (1 + len(parts)),
        out_shape=[jax.ShapeDtypeStruct((rows, width), BF16)] * 2,
        compiler_params=pltpu.CompilerParams(vmem_limit_bytes=VMEM),
        name="last_sum",
    )(held(bias), *[held(part) for part in parts])


def levels_of(devices):
    levels = [(1, 2)] if devices > 1 else []
    unit = 2
    if (devices.bit_length() - 1) % 2 == 0 and devices > 2:
        levels.append((unit, 2))
        unit *= 2
    while unit < devices:
        levels.append((unit, 4))
        unit *= 4
    return levels


def shards(tokens, weight_hidden, bias_hidden, weight_output, bias_output, cotangent):
    devices = lax.axis_size("gx")
    position = lax.axis_index("gx")
    narrow = weight_hidden.shape[1]
    width = tokens.shape[1]
    levels = levels_of(devices)

    def swap(value, step):
        return lax.ppermute(value, "gx", [(i, i ^ step) for i in range(devices)])

    mine = jnp.stack([tokens, cotangent])
    for unit, size in reversed(levels[1:]):
        mine = jnp.concatenate([mine] + [swap(mine, unit * j) for j in range(1, size)], axis=1)
    bias = lax.dynamic_slice(bias_hidden, (position * narrow,), (narrow,)).reshape(1, narrow)
    theirs = swap(mine, 1)

    tile = width // STEPS
    done = PASS
    beside = [0] + [HOP] * (len(levels) - 2)
    beside.append(STEPS - done - sum(beside))
    (active, grad_hidden, grad_bias_hidden, grad_bias_output, both, keep, send, grad_weight_hidden,
     grad_weight_output) = weights_pass(mine, theirs, bias, weight_hidden, weight_output, done * tile)

    sends = [send]
    for k, (unit, size) in enumerate(levels):
        arrived = [swap(piece, unit * (j + 1)) for j, piece in enumerate(sends)]
        if beside[k]:
            grad_weight_hidden, grad_weight_output = outer_rows(
                both, active, grad_hidden, grad_weight_hidden, grad_weight_output, done, beside[k], tile
            )
            done += beside[k]
        if k + 1 < len(levels):
            keep, *sends = add_and_split(grad_weight_output, [keep] + arrived, levels[k + 1][1])
    layer_output, grad_tokens = last_sum(bias_output.reshape(1, width), [keep] + arrived)
    return (
        layer_output,
        grad_tokens,
        grad_weight_hidden,
        grad_bias_hidden.reshape(narrow),
        grad_weight_output,
        grad_bias_output.reshape(width),
    )


def solution(mesh):
    in_specs = (
        P(("grp", "gx"), None),
        P(None, "gx"),
        P(),
        P(None, "gx"),
        P(),
        P(("grp", "gx"), None),
    )
    out_specs = (
        P(("grp", "gx"), None),
        P(("grp", "gx"), None),
        P(None, ("grp", "gx")),
        P(("grp", "gx")),
        P(None, ("grp", "gx")),
        P("grp"),
    )
    return jax.shard_map(shards, mesh=mesh, in_specs=in_specs, out_specs=out_specs, check_vma=False)
```

time: 95.9 us -> 79.1 us (0.82); the launches traced: 94.6 us -> 78.9 us
  Pallas kernels: 58.4 us -> 48.6 us
  local copies, waits for them, and re-layouts: 7.51 us -> 1.15 us
  other arithmetic: 4.11 us -> 1.81 us
  waiting for transfers between devices: 11.2 us -> 13.2 us
    pallas_call x3 -> x6, Pallas kernels: 58.4 us -> 48.6 us  [the longest x1 34.1 us: weights_pass(): pl.pallas_call(weights_body, grid=(units // tile,), in_specs=[HELD, HELD,...]
    concatenate x2 -> x1, local copies, waits for them, and re-layouts: 3.44 us -> 0.43 us  [shards(): jnp.concatenate([mine] + [swap(mine, unit * j) for j in range(1, size)],...]
    ppermute x10, waiting for transfers between devices: 11.2 us -> 13.2 us  [swap(): return lax.ppermute(value, 'gx', [(i, i ^ step) for i in range(devices)])]
    add x3 -> x0, other arithmetic: 1.51 us -> none  [shards(): partial = partial + piece.astype(F32)]
    squeeze x1 -> x0, local copies, waits for them, and re-layouts: 1.19 us -> none  [shards(): pieces[:, j].astype(kind)]
  transfers between devices with their start and end apart: 10 -> 10, of which waited for: 5 -> 5; matrix products, arithmetic and copies ran while one was open for 1% -> 1% of each run, Pallas kernels for 30% -> 17%
where the time goes in v2:
time: 79.1 us; the launch traced here: 78.9 us
  Pallas kernels  48.6 us (61%)
  starting transfers between devices  13.4 us (17%)
  waiting for transfers between devices  13.2 us (17%)
  other arithmetic  1.81 us (2%)
  local copies, waits for them, and re-layouts  1.15 us (1%)
    pallas_call x1, Pallas kernels, weights_pass(): pl.pallas_call(weights_body, grid=(units // tile,), in_specs=[HELD, HELD,...  34.1 us
    pallas_call x2, Pallas kernels, outer_rows(): pl.pallas_call(functools.partial(outer_body, first), grid=(steps,), in_sp...  13.6 us
    ppermute x10, starting transfers between devices, swap(): return lax.ppermute(value, 'gx', [(i, i ^ step) for i in range(devices)])  13.4 us
    ppermute x10, waiting for transfers between devices, swap(): return lax.ppermute(value, 'gx', [(i, i ^ step) for i in range(devices)])  13.2 us
  transfers between devices with their start and end apart: 10, of which 5 were waited for; matrix products, arithmetic and copies ran while one was open for 1% of the time, Pallas kernels for 17%

profile of v2, /device:TPU:0, one launch (start us, length us, event | category | flops | bytes accessed | tf_op | source)
XLA Modules:
  0.0 78.9 jit_solution(13670087048604779908)
XLA Ops:
  0.6 0.8 %pad_maximum_fusion.1 = bf16[2,2,6144]{2,1,0:T(2,128)(2,1)S(1)} fusion(bf16[1,2,6144]{2,1,0:T(2,128)(2,1)} %bitcast.4, bf16[1,2,6144]{2,1,0:T(2,128)(2,1)} %bitcast.6), kind=kLoop, calls=%fused_computation.1 | loop fusion | flops 24576 | bytes 98304 | tf_op jit(solution)/shard_map/stack | solution.py:217
  1.5 3.1 %collective-permute-start = (bf16[2,2,6144]{2,1,0:T(2,128)(2,1)S(1)}, bf16[2,2,6144]{2,1,0:T(2,128)(2,1)S(1)}, u32[]{:S(2)}, u32[]{:S(2)}) collective-permute-start(bf16[2,2,6144]{2,1,0:T(2,128)(2,1)S(1)} %pad_maximum_fusion.1), channel_id=1, source_target_pairs={{0,4},{1,5},{2,6},{3,7},{4,0},{5,1},{6,2},{7,3},{8,12},{9,13},{10,... | collective-permute-start | bytes 147464 | tf_op jit(solution)/shard_map/ppermute | solution.py:215
  4.6 2.6 %collective-permute-start.1 = (bf16[2,2,6144]{2,1,0:T(2,128)(2,1)S(1)}, bf16[2,2,6144]{2,1,0:T(2,128)(2,1)S(1)}, u32[]{:S(2)}, u32[]{:S(2)}) collective-permute-start(bf16[2,2,6144]{2,1,0:T(2,128)(2,1)S(1)} %pad_maximum_fusion.1), channel_id=1, source_target_pairs={{0,8},{1,9},{2,10},{3,11},{4,12},{5,13},{6,14},{7,15},{8,0},{9,1},... | collective-permute-start | bytes 147464 | tf_op jit(solution)/shard_map/ppermute | solution.py:215
  7.1 3.3 %collective-permute-done.1 = bf16[2,2,6144]{2,1,0:T(2,128)(2,1)S(1)} collective-permute-done((bf16[2,2,6144]{2,1,0:T(2,128)(2,1)S(1)}, bf16[2,2,6144]{2,1,0:T(2,128)(2,1)S(1)}, u32[]{:S(2)}, u32[]{:S(2)}) %collective-permute-start.1) | collective-permute-done | bytes 49184 | tf_op jit(solution)/shard_map/ppermute | solution.py:215
  10.5 2.6 %collective-permute-done.2 = bf16[2,2,6144]{2,1,0:T(2,128)(2,1)S(1)} collective-permute-done((bf16[2,2,6144]{2,1,0:T(2,128)(2,1)S(1)}, bf16[2,2,6144]{2,1,0:T(2,128)(2,1)S(1)}, u32[]{:S(2)}, u32[]{:S(2)}) %collective-permute-start.2) | collective-permute-done | bytes 49184 | tf_op jit(solution)/shard_map/ppermute | solution.py:215
  13.0 1.0 %pad_maximum_fusion = bf16[2,8,6144]{2,1,0:T(8,128)(2,1)S(1)} fusion(bf16[2,2,6144]{2,1,0:T(2,128)(2,1)S(1)} %collective-permute-done.2, bf16[2,2,6144]{2,1,0:T(2,128)(2,1)S(1)} %collective-permute-done.1, bf16[2,2,6144]{2,1,0:T(2,128)(2,1)S(1)} %collective-permute-done, bf16[1,2,6144]{2,1,0:T(2,128)(2,1)} %bitcast.5, bf16[1,2,6144]{2,1,0:T(2,128)(2,1)} %bitcast.7), kind=kLoop, calls=%fused_computation | loop fusion | flops 983040 | bytes 393216 | tf_op jit(solution)/shard_map/concatenate | solution.py:219
  14.0 1.6 %collective-permute-start.3 = (bf16[2,8,6144]{2,1,0:T(8,128)(2,1)S(1)}, bf16[2,8,6144]{2,1,0:T(8,128)(2,1)S(1)}, u32[]{:S(2)}, u32[]{:S(2)}) collective-permute-start(bf16[2,8,6144]{2,1,0:T(8,128)(2,1)S(1)} %pad_maximum_fusion), channel_id=1, source_target_pairs={{0,2},{1,3},{2,0},{3,1},{4,6},{5,7},{6,4},{7,5},{8,10},{9,11},{10,... | collective-permute-start | bytes 589832 | tf_op jit(solution)/shard_map/ppermute | solution.py:215
  15.6 4.2 %collective-permute-done.3 = bf16[2,8,6144]{2,1,0:T(8,128)(2,1)S(1)} collective-permute-done((bf16[2,8,6144]{2,1,0:T(8,128)(2,1)S(1)}, bf16[2,8,6144]{2,1,0:T(8,128)(2,1)S(1)}, u32[]{:S(2)}, u32[]{:S(2)}) %collective-permute-start.3) | collective-permute-done | bytes 196640 | tf_op jit(solution)/shard_map/ppermute | solution.py:215
  19.7 0.4 concatenate.8.mine
  20.2 0.1 collective-permute-start.4
  20.3 0.7 dynamic_slice.3
  21.0 1.0 %collective-permute-done.4.theirs = bf16[2,16,6144]{2,1,0:T(8,128)(2,1)S(1)} collective-permute-done((bf16[2,16,6144]{2,1,0:T(8,128)(2,1)S(1)}, bf16[2,16,6144]{2,1,0:T(8,128)(2,1)S(1)}, u32[]{:S(2)}, u32[]{:S(2)}) %collective-permute-start.4) | collective-permute-done | bytes 393248 | tf_op jit(solution)/shard_map/ppermute | solution.py:215
  22.0 34.1 %weights_pass.1 = (bf16[32,2048]{1,0:T(8,128)(2,1)S(1)}, bf16[32,2048]{1,0:T(8,128)(2,1)S(1)}, f32[1,2048]{1,0:T(1,128)}, f32[1,6144]{1,0:T(1,128)}, bf16[2,32,6...) custom-call(bf16[2,16,6144]{2,1,0:T(8,128)(2,1)S(1)} %concatenate.8., ...), custom_call_target="tpu_custom_call" | custom-call | flops 4831838208 | bytes 75497472 | tf_op jit(solution)/shard_map/weights_pass/pallas_call | solution.py:78
  56.1 0.1 collective-permute-start.5
  56.2 2.2 %collective-permute-done.5.refs_1_ = f32[2,16,6144]{2,1,0:T(8,128)S(1)} collective-permute-done((f32[2,16,6144]{2,1,0:T(8,128)S(1)}, f32[2,16,6144]{2,1,0:T(8,128)S(1)}, u32[]{:S(2)}, u32[]{:S(2)}) %collective-permute-start.5) | collective-permute-done | bytes 786464 | tf_op jit(solution)/shard_map/ppermute | solution.py:215
  58.4 0.1 add_and_split.2
  58.5 1.6 %collective-permute-start.6 = (bf16[2,8,6144]{2,1,0:T(8,128)(2,1)S(1)}, bf16[2,8,6144]{2,1,0:T(8,128)(2,1)S(1)}, u32[]{:S(2)}, u32[]{:S(2)}) collective-permute-start(bf16[2,8,6144]{2,1,0:T(8,128)(2,1)S(1)} %get-tuple-element.36), channel_id=1, source_target_pairs={{0,2},{1,3},{2,0},{3,1},{4,6},{5,7},{6,4},{7,5},{8,10},{9,11},{10,... | collective-permute-start | bytes 589832 | tf_op jit(solution)/shard_map/ppermute | solution.py:215
  60.1 5.4 %outer_rows.2 = (bf16[6144,2048]{1,0:T(8,128)(2,1)}, bf16[6144,2048]{1,0:T(8,128)(2,1)}) custom-call(bf16[2,32,6144]{2,1,0:T(8,128)(2,1)S(1)} %get-tuple-element.27.both, bf16[32,2048]{1,0:T(8,128)(2,1)S(1)} %get-tuple-element.28.active, bf16[32,2048]{1,0:T(8,128)(2,1)S(1)} %get-tuple-element.29.grad_hidden, ...), custom_call_target="tpu_custom_call", output_to_operand_aliasing={{0}: (3, {}), {1}: (4, {})} | custom-call | flops 402653184 | bytes 12582912 | tf_op jit(solution)/shard_map/outer_rows/pallas_call | solution.py:131
  65.5 0.1 add_and_split.3
  65.6 0.1 collective-permute-start.7
  65.7 1.3 %collective-permute-start.8 = (bf16[2,2,6144]{2,1,0:T(2,128)(2,1)S(1)}, bf16[2,2,6144]{2,1,0:T(2,128)(2,1)S(1)}, u32[]{:S(2)}, u32[]{:S(2)}) collective-permute-start(bf16[2,2,6144]{2,1,0:T(2,128)(2,1)S(1)} %get-tuple-element.39), channel_id=1, source_target_pairs={{0,8},{1,9},{2,10},{3,11},{4,12},{5,13},{6,14},{7,15},{8,0},{9,1},... | collective-permute-start | bytes 147464 | tf_op jit(solution)/shard_map/ppermute | solution.py:215
  67.0 3.1 %collective-permute-start.9 = (bf16[2,2,6144]{2,1,0:T(2,128)(2,1)S(1)}, bf16[2,2,6144]{2,1,0:T(2,128)(2,1)S(1)}, u32[]{:S(2)}, u32[]{:S(2)}) collective-permute-start(bf16[2,2,6144]{2,1,0:T(2,128)(2,1)S(1)} %get-tuple-element.40), channel_id=1, source_target_pairs={{0,12},{1,13},{2,14},{3,15},{4,8},{5,9},{6,10},{7,11},{8,4},{9,5},... | collective-permute-start | bytes 147464 | tf_op jit(solution)/shard_map/ppermute | solution.py:215
  70.1 8.1 %outer_rows.3 = (bf16[6144,2048]{1,0:T(8,128)(2,1)}, bf16[6144,2048]{1,0:T(8,128)(2,1)}) custom-call(bf16[2,32,6144]{2,1,0:T(8,128)(2,1)S(1)} %get-tuple-element.27.both, bf16[32,2048]{1,0:T(8,128)(2,1)S(1)} %get-tuple-element.28.active, bf16[32,2048]{1,0:T(8,128)(2,1)S(1)} %get-tuple-element.29.grad_hidden, ...), custom_call_target="tpu_custom_call", output_to_operand_aliasing={{0}: (3, {}), {1}: (4, {})} | custom-call | flops 671088640 | bytes 20971520 | tf_op jit(solution)/shard_map/outer_rows/pallas_call | solution.py:131
  78.2 0.7 last_sum.1
  (10 shorter events, 0.0 us)
Async XLA Ops:
  1.5 5.7 %collective-permute-start = (bf16[2,2,6144]{2,1,0:T(2,128)(2,1)S(1)}, bf16[2,2,6144]{2,1,0:T(2,128)(2,1)S(1)}, u32[]{:S(2)}, u32[]{:S(2)}) collective-permute-start(bf16[2,2,6144]{2,1,0:T(2,128)(2,1)S(1)} %pad_maximum_fusion.1), channel_id=1, source_target_pairs={{0,4},{1,5},{2,6},{3,7},{4,0},{5,1},{6,2},{7,3},{8,12},{9,13},{10,... | collective-permute-start | bytes 147464 | tf_op jit(solution)/shard_map/ppermute | solution.py:215
  4.6 5.9 %collective-permute-start.1 = (bf16[2,2,6144]{2,1,0:T(2,128)(2,1)S(1)}, bf16[2,2,6144]{2,1,0:T(2,128)(2,1)S(1)}, u32[]{:S(2)}, u32[]{:S(2)}) collective-permute-start(bf16[2,2,6144]{2,1,0:T(2,128)(2,1)S(1)} %pad_maximum_fusion.1), channel_id=1, source_target_pairs={{0,8},{1,9},{2,10},{3,11},{4,12},{5,13},{6,14},{7,15},{8,0},{9,1},... | collective-permute-start | bytes 147464 | tf_op jit(solution)/shard_map/ppermute | solution.py:215
  7.1 5.9 %collective-permute-start.2 = (bf16[2,2,6144]{2,1,0:T(2,128)(2,1)S(1)}, bf16[2,2,6144]{2,1,0:T(2,128)(2,1)S(1)}, u32[]{:S(2)}, u32[]{:S(2)}) collective-permute-start(bf16[2,2,6144]{2,1,0:T(2,128)(2,1)S(1)} %pad_maximum_fusion.1), channel_id=1, source_target_pairs={{0,12},{1,13},{2,14},{3,15},{4,8},{5,9},{6,10},{7,11},{8,4},{9,5},... | collective-permute-start | bytes 147464 | tf_op jit(solution)/shard_map/ppermute | solution.py:215
  14.0 5.7 %collective-permute-start.3 = (bf16[2,8,6144]{2,1,0:T(8,128)(2,1)S(1)}, bf16[2,8,6144]{2,1,0:T(8,128)(2,1)S(1)}, u32[]{:S(2)}, u32[]{:S(2)}) collective-permute-start(bf16[2,8,6144]{2,1,0:T(8,128)(2,1)S(1)} %pad_maximum_fusion), channel_id=1, source_target_pairs={{0,2},{1,3},{2,0},{3,1},{4,6},{5,7},{6,4},{7,5},{8,10},{9,11},{10,... | collective-permute-start | bytes 589832 | tf_op jit(solution)/shard_map/ppermute | solution.py:215
  20.2 1.8 %collective-permute-start.4 = (bf16[2,16,6144]{2,1,0:T(8,128)(2,1)S(1)}, bf16[2,16,6144]{2,1,0:T(8,128)(2,1)S(1)}, u32[]{:S(2)}, u32[]{:S(2)}) collective-permute-start(bf16[2,16,6144]{2,1,0:T(8,128)(2,1)S(1)} %concatenate.8.mine), channel_id=1, source_target_pairs={{0,1},{1,0},{2,3},{3,2},{4,5},{5,4},{6,7},{7,6},{8,9},{9,8},{10,11... | collective-permute-start | bytes 1179656 | tf_op jit(solution)/shard_map/ppermute | solution.py:215
  56.1 4.0 %copy-start = (bf16[6144]{0:T(1024)(128)(2,1)S(1)}, bf16[6144]{0:T(1024)(128)(2,1)}, u32[]{:S(2)}) copy-start(bf16[6144]{0:T(1024)(128)(2,1)} %param.10) | copy-start | bytes 36868
  56.1 2.3 %collective-permute-start.5 = (f32[2,16,6144]{2,1,0:T(8,128)S(1)}, f32[2,16,6144]{2,1,0:T(8,128)S(1)}, u32[]{:S(2)}, u32[]{:S(2)}) collective-permute-start(f32[2,16,6144]{2,1,0:T(8,128)S(1)} %get-tuple-element.34), channel_id=1, source_target_pairs={{0,1},{1,0},{2,3},{3,2},{4,5},{5,4},{6,7},{7,6},{8,9},{9,8},{10,11... | collective-permute-start | bytes 2359304 | tf_op jit(solution)/shard_map/ppermute | solution.py:215
  58.5 7.0 %collective-permute-start.6 = (bf16[2,8,6144]{2,1,0:T(8,128)(2,1)S(1)}, bf16[2,8,6144]{2,1,0:T(8,128)(2,1)S(1)}, u32[]{:S(2)}, u32[]{:S(2)}) collective-permute-start(bf16[2,8,6144]{2,1,0:T(8,128)(2,1)S(1)} %get-tuple-element.36), channel_id=1, source_target_pairs={{0,2},{1,3},{2,0},{3,1},{4,6},{5,7},{6,4},{7,5},{8,10},{9,11},{10,... | collective-permute-start | bytes 589832 | tf_op jit(solution)/shard_map/ppermute | solution.py:215
  65.6 12.6 %collective-permute-start.7 = (bf16[2,2,6144]{2,1,0:T(2,128)(2,1)S(1)}, bf16[2,2,6144]{2,1,0:T(2,128)(2,1)S(1)}, u32[]{:S(2)}, u32[]{:S(2)}) collective-permute-start(bf16[2,2,6144]{2,1,0:T(2,128)(2,1)S(1)} %get-tuple-element.38), channel_id=1, source_target_pairs={{0,4},{1,5},{2,6},{3,7},{4,0},{5,1},{6,2},{7,3},{8,12},{9,13},{10,... | collective-permute-start | bytes 147464 | tf_op jit(solution)/shard_map/ppermute | solution.py:215
  65.7 12.5 %collective-permute-start.8 = (bf16[2,2,6144]{2,1,0:T(2,128)(2,1)S(1)}, bf16[2,2,6144]{2,1,0:T(2,128)(2,1)S(1)}, u32[]{:S(2)}, u32[]{:S(2)}) collective-permute-start(bf16[2,2,6144]{2,1,0:T(2,128)(2,1)S(1)} %get-tuple-element.39), channel_id=1, source_target_pairs={{0,8},{1,9},{2,10},{3,11},{4,12},{5,13},{6,14},{7,15},{8,0},{9,1},... | collective-permute-start | bytes 147464 | tf_op jit(solution)/shard_map/ppermute | solution.py:215
  67.0 11.2 %collective-permute-start.9 = (bf16[2,2,6144]{2,1,0:T(2,128)(2,1)S(1)}, bf16[2,2,6144]{2,1,0:T(2,128)(2,1)S(1)}, u32[]{:S(2)}, u32[]{:S(2)}) collective-permute-start(bf16[2,2,6144]{2,1,0:T(2,128)(2,1)S(1)} %get-tuple-element.40), channel_id=1, source_target_pairs={{0,12},{1,13},{2,14},{3,15},{4,8},{5,9},{6,10},{7,11},{8,4},{9,5},... | collective-permute-start | bytes 147464 | tf_op jit(solution)/shard_map/ppermute | solution.py:215

commit v3 on v2

--- a/solution.py
+++ b/solution.py
@@ -12,15 +12,21 @@
 BF16 = jnp.bfloat16
 SCALE = math.sqrt(2.0 / math.pi)
 CUBE = 0.044715
-VMEM = 34 * 2**20
-STEPS = 12
-PASS = 4
-HOP = 3
+VMEM = 24 * 2**20
+STEPS = 24
+PASS = 6
+CORE = 2
+HOP = 8
 HELD = pl.BlockSpec(memory_space=pltpu.VMEM)
+FAR = pl.BlockSpec(memory_space=pltpu.HBM)
 
 
 def held(value):
     return pltpu.with_memory_space_constraint(value, pltpu.VMEM)
+
+
+def far(value):
+    return pltpu.with_memory_space_constraint(value, pltpu.HBM)
 
 
 def product(left, right, dims):
@@ -35,10 +41,80 @@
     return value * half, slope
 
 
-def weights_body(mine, theirs, bias, weight_hidden, weight_output, active, grad_hidden, grad_bias_hidden,
-                 grad_bias_output, both, keep, send, grad_weight_hidden, grad_weight_output, turned):
+def tile_of(units, count):
+    return min(256 if count <= 64 else 128, units)
+
+
+def fetch(weights, which, slots, arrived):
+    slot = which % 2 if isinstance(which, int) else lax.rem(which, 2)
+    tile = slots.shape[-1]
+    at = which * tile
+    place = pl.ds(at if isinstance(which, int) else pl.multiple_of(at, tile), tile)
+    return [
+        pltpu.make_async_copy(weight.at[:, place], slots.at[slot, k], arrived.at[slot, k])
+        for k, weight in enumerate(weights)
+    ]
+
+
+def first_body(_mine, _bias, weight_hidden, weight_output, slots, mark, arrived):
+    mark[...] = jnp.zeros_like(mark)
+    copies = fetch((weight_hidden, weight_output), 0, slots, arrived)
+    for copy in copies:
+        copy.start()
+    for copy in copies:
+        copy.wait()
+
+
+def first_tiles(after, weight_hidden, weight_output, tile):
+    width = weight_hidden.shape[0]
+    return pl.pallas_call(
+        first_body,
+        in_specs=[HELD, HELD, FAR, FAR],
+        out_specs=[HELD, HELD],
+        out_shape=[pltpu.VMEM((2, 2, width, tile), BF16), pltpu.VMEM((8, 128), F32)],
+        scratch_shapes=[pltpu.SemaphoreType.DMA((2, 2))],
+        compiler_params=pltpu.CompilerParams(vmem_limit_bytes=2**20),
+        cost_estimate=pl.CostEstimate(flops=0, bytes_accessed=4 * width * tile, transcendentals=0),
+        name="first_tiles",
+    )(*[held(value) for value in after], far(weight_hidden), far(weight_output))
+
+
+def join_body(number, *refs):
+    parts, result = refs[:number][::-1], refs[-1]
+    result[...] = jnp.concatenate([part[...].astype(F32) for part in parts], axis=1).astype(BF16)
+
+
+def join(parts, after=()):
+    operands = list(parts)[::-1] + list(after)
+    kind, rows, width = parts[0].shape
+    return pl.pallas_call(
+        functools.partial(join_body, len(parts)),
+        in_specs=[HELD] * len(operands),
+        out_specs=HELD,
+        out_shape=pltpu.VMEM((kind, rows * len(parts), width), BF16),
+        compiler_params=pltpu.CompilerParams(vmem_limit_bytes=VMEM),
+        name="join",
+    )(*[held(operand) for operand in operands])
+
+
+def weights_body(mine, theirs, bias, weight_hidden, weight_output, _slots, active, grad_hidden, grad_bias_hidden,
+                 grad_bias_output, both, keep, send, grad_weight_hidden, grad_weight_output, slots, turned, arrived):
     near = mine.shape[1]
     rows, tile = grad_weight_output.shape
+    step = pl.program_id(0)
+    steps = pl.num_programs(0)
+    weights = (weight_hidden, weight_output)
+
+    @pl.when(step >= 1)
+    def _():
+        for copy in fetch(weights, step, slots, arrived):
+            copy.wait()
+
+    @pl.when(step + 1 < steps)
+    def _():
+        for copy in fetch(weights, step + 1, slots, arrived):
+            copy.start()
+
 
     @pl.when(pl.program_id(0) == 0)
     def _():
@@ -50,30 +126,32 @@
         turned[0] = both[0, :, :rows].T
         turned[1] = both[1, :, :rows].T
 
-    hidden = product(both[0], weight_hidden[...], ((1,), (0,))) + bias[...].astype(F32)
+    slot = lax.rem(step, 2)
+    weight_hidden = slots[slot, 0]
+    weight_output = slots[slot, 1]
+    place = pl.ds(pl.multiple_of(step * tile, tile), tile)
+    hidden = product(both[0], weight_hidden, ((1,), (0,))) + bias[:, place].astype(F32)
     value, slope = gelu_and_slope(hidden)
     value = value.astype(BF16)
-    at = pl.program_id(0) * tile
-    place = pl.ds(pl.multiple_of(at, tile), tile)
     active[:, place] = value
-    grad = (product(both[1], weight_output[...], ((1,), (0,))) * slope).astype(BF16)
+    grad = (product(both[1], weight_output, ((1,), (0,))) * slope).astype(BF16)
     grad_hidden[:, place] = grad
     grad_bias_hidden[...] = jnp.sum(grad.astype(F32), axis=0, keepdims=True)
-    share = product(value, weight_output[...], ((1,), (1,)))
+    share = product(value, weight_output, ((1,), (1,)))
     keep[0] += share[:near]
     send[0] += share[near:]
-    share = product(grad, weight_hidden[...], ((1,), (1,)))
+    share = product(grad, weight_hidden, ((1,), (1,)))
     keep[1] += share[:near]
     send[1] += share[near:]
     grad_weight_hidden[...] = product(turned[0], grad, ((1,), (0,))).astype(BF16)
     grad_weight_output[...] = product(turned[1], value, ((1,), (0,))).astype(BF16)
 
 
-def weights_pass(mine, theirs, bias, weight_hidden, weight_output, rows):
+def weights_pass(mine, theirs, bias, weight_hidden, weight_output, slots, rows):
     _, near, width = mine.shape
     count = 2 * near
     units = weight_hidden.shape[1]
-    tile = min(256 if count <= 64 else 128, units)
+    tile = slots.shape[-1]
     across = lambda i: (0, i)
     return pl.pallas_call(
         weights_body,
@@ -81,9 +159,10 @@
         in_specs=[
             HELD,
             HELD,
-            pl.BlockSpec((1, tile), across),
-            pl.BlockSpec((width, tile), across),
-            pl.BlockSpec((width, tile), across),
+            HELD,
+            FAR,
+            FAR,
+            HELD,
         ],
         out_specs=[
             HELD,
@@ -95,6 +174,7 @@
             HELD,
             pl.BlockSpec((rows, tile), across),
             pl.BlockSpec((rows, tile), across),
+            HELD,
         ],
         out_shape=[
             pltpu.VMEM((count, units), BF16),
@@ -106,17 +186,20 @@
             pltpu.VMEM((2, near, width), F32),
             jax.ShapeDtypeStruct((width, units), BF16),
             jax.ShapeDtypeStruct((width, units), BF16),
+            pltpu.VMEM(slots.shape, BF16),
         ],
-        scratch_shapes=[pltpu.VMEM((2, rows, count), BF16)],
+        input_output_aliases={5: 9},
+        scratch_shapes=[pltpu.VMEM((2, rows, count), BF16), pltpu.SemaphoreType.DMA((2, 2))],
         compiler_params=pltpu.CompilerParams(vmem_limit_bytes=VMEM),
         cost_estimate=pl.CostEstimate(
             flops=12 * count * width * units, bytes_accessed=6 * width * units, transcendentals=count * units
         ),
         name="weights_pass",
-    )(held(mine), held(theirs), bias, weight_hidden, weight_output)
-
-
-def outer_body(first, both, active, grad_hidden, _hidden, _output, grad_weight_hidden, grad_weight_output):
+    )(held(mine), held(theirs), held(bias), far(weight_hidden), far(weight_output), held(slots))
+
+
+def outer_body(first, both, active, grad_hidden, _hidden, _output, grad_weight_hidden, grad_weight_output, mark):
+    mark[...] = jnp.zeros_like(mark)
     tile = grad_weight_output.shape[0]
     at = (first + pl.program_id(0)) * tile
     place = pl.ds(pl.multiple_of(at, tile), tile)
@@ -135,18 +218,18 @@
             HELD,
             HELD,
             HELD,
-            pl.BlockSpec(memory_space=pl.ANY),
-            pl.BlockSpec(memory_space=pl.ANY),
+            FAR,
+            FAR,
         ],
-        out_specs=[place, place],
-        out_shape=[jax.ShapeDtypeStruct((width, units), BF16)] * 2,
+        out_specs=[place, place, HELD],
+        out_shape=[jax.ShapeDtypeStruct((width, units), BF16)] * 2 + [pltpu.VMEM((8, 128), F32)],
         input_output_aliases={3: 0, 4: 1},
         compiler_params=pltpu.CompilerParams(vmem_limit_bytes=VMEM),
         cost_estimate=pl.CostEstimate(
             flops=4 * count * steps * tile * units, bytes_accessed=4 * steps * tile * units, transcendentals=0
         ),
         name="outer_rows",
-    )(held(both), held(active), held(grad_hidden), grad_weight_hidden, grad_weight_output)
+    )(held(both), held(active), held(grad_hidden), far(grad_weight_hidden), far(grad_weight_output))
 
 
 def split_body(size, _after, *refs):
@@ -164,12 +247,12 @@
     cut = (2, rows // size, width)
     return pl.pallas_call(
         functools.partial(split_body, size),
-        in_specs=[pl.BlockSpec(memory_space=pl.ANY)] + [HELD] * len(parts),
+        in_specs=[HELD] * (1 + len(parts)),
         out_specs=[HELD] * size,
         out_shape=[pltpu.VMEM(cut, F32)] + [pltpu.VMEM(cut, BF16)] * (size - 1),
         compiler_params=pltpu.CompilerParams(vmem_limit_bytes=VMEM),
         name="add_and_split",
-    )(after, *[held(part) for part in parts])
+    )(*[held(part) for part in [after] + parts])
 
 
 def last_body(bias, *refs):
@@ -215,28 +298,38 @@
         return lax.ppermute(value, "gx", [(i, i ^ step) for i in range(devices)])
 
     mine = jnp.stack([tokens, cotangent])
+    count = tokens.shape[0] * devices
+    bias = lax.dynamic_slice(bias_hidden, (position * narrow,), (narrow,)).reshape(1, narrow)
     for unit, size in reversed(levels[1:]):
-        mine = jnp.concatenate([mine] + [swap(mine, unit * j) for j in range(1, size)], axis=1)
-    bias = lax.dynamic_slice(bias_hidden, (position * narrow,), (narrow,)).reshape(1, narrow)
+        arrived = [swap(mine, unit * j) for j in range(1, size)]
+        after = [bias]
+        if unit == 2:
+            slots, mark = first_tiles([mine, bias], weight_hidden, weight_output, tile_of(narrow, count))
+            after = [mark]
+        mine = join([mine] + arrived, after)
     theirs = swap(mine, 1)
 
-    tile = width // STEPS
+    part = width // STEPS
     done = PASS
-    beside = [0] + [HOP] * (len(levels) - 2)
+    beside = [CORE] + [HOP] * (len(levels) - 2)
     beside.append(STEPS - done - sum(beside))
     (active, grad_hidden, grad_bias_hidden, grad_bias_output, both, keep, send, grad_weight_hidden,
-     grad_weight_output) = weights_pass(mine, theirs, bias, weight_hidden, weight_output, done * tile)
+     grad_weight_output, _) = weights_pass(
+         mine, theirs, bias, weight_hidden, weight_output, slots, done * part
+    )
 
     sends = [send]
     for k, (unit, size) in enumerate(levels):
         arrived = [swap(piece, unit * (j + 1)) for j, piece in enumerate(sends)]
         if beside[k]:
-            grad_weight_hidden, grad_weight_output = outer_rows(
-                both, active, grad_hidden, grad_weight_hidden, grad_weight_output, done, beside[k], tile
+            wide = 2 if beside[k] % 2 == 0 and done % 2 == 0 and k > 0 else 1
+            grad_weight_hidden, grad_weight_output, mark = outer_rows(
+                both, active, grad_hidden, grad_weight_hidden, grad_weight_output, done // wide, beside[k] // wide,
+                part * wide
             )
             done += beside[k]
         if k + 1 < len(levels):
-            keep, *sends = add_and_split(grad_weight_output, [keep] + arrived, levels[k + 1][1])
+            keep, *sends = add_and_split(mark, [keep] + arrived, levels[k + 1][1])
     layer_output, grad_tokens = last_sum(bias_output.reshape(1, width), [keep] + arrived)
     return (
         layer_output,

time: 79.1 us -> 72.7 us (0.919)
  waiting for transfers between devices: 13.2 us -> 6.73 us
  Pallas kernels: 48.6 us -> 49.9 us
  other arithmetic: 1.81 us -> 0.83 us
    ppermute x10, waiting for transfers between devices: 13.2 us -> 6.73 us  [swap(): return lax.ppermute(value, 'gx', [(i, i ^ step) for i in range(devices)])]
    pallas_call x1, Pallas kernels: 34.1 us -> 29.9 us  [weights_pass(): pl.pallas_call(weights_body, grid=(units // tile,), in_specs=[HELD, HELD,...]
    pallas_call x2 -> x5, Pallas kernels: 0.2 us -> 3.24 us  [the longest x1 2.89 us: first_tiles(): pl.pallas_call(first_body, in_specs=[HELD, HELD, FAR, FAR], out_specs=[HE...]
    pallas_call x2 -> x3, Pallas kernels: 13.6 us -> 16 us  [outer_rows(): pl.pallas_call(functools.partial(outer_body, first), grid=(steps,), in_sp...]
    concatenate x1 -> x0, other arithmetic: 0.98 us -> none  [shards(): jnp.concatenate([mine] + [swap(mine, unit * j) for j in range(1, size)],...]
  transfers between devices with their start and end apart: 10 -> 10, of which waited for: 5 -> 4; matrix products, arithmetic and copies ran while one was open for 1% -> 1% of each run, Pallas kernels for 17% -> 26%
where the time goes in v3:
time: 72.7 us; the launch traced here: 72.4 us
  Pallas kernels  49.9 us (69%)
  starting transfers between devices  13.6 us (19%)
  waiting for transfers between devices  6.73 us (9%)
  other arithmetic  0.83 us (1%)
    pallas_call x1, Pallas kernels, weights_pass(): pl.pallas_call(weights_body, grid=(units // tile,), in_specs=[HELD, HELD,...  29.9 us
    pallas_call x3, Pallas kernels, outer_rows(): pl.pallas_call(functools.partial(outer_body, first), grid=(steps,), in_sp...  16 us
    ppermute x10, starting transfers between devices, swap(): return lax.ppermute(value, 'gx', [(i, i ^ step) for i in range(devices)])  13.6 us
    ppermute x10, waiting for transfers between devices, swap(): return lax.ppermute(value, 'gx', [(i, i ^ step) for i in range(devices)])  6.73 us
    pallas_call x1, Pallas kernels, first_tiles(): pl.pallas_call(first_body, in_specs=[HELD, HELD, FAR, FAR], out_specs=[HE...  2.89 us
  transfers between devices with their start and end apart: 10, of which 4 were waited for; matrix products, arithmetic and copies ran while one was open for 1% of the time, Pallas kernels for 26%

profile of v3, /device:TPU:0, one launch (start us, length us, event | category | flops | bytes accessed | tf_op | source)
XLA Modules:
  0.0 72.4 jit_solution(9941512185759282029)
XLA Ops:
  0.6 0.8 %pad_maximum_fusion.refs_3_ = bf16[2,2,6144]{2,1,0:T(2,128)(2,1)S(1)} fusion(bf16[1,2,6144]{2,1,0:T(2,128)(2,1)} %bitcast.4, bf16[1,2,6144]{2,1,0:T(2,128)(2,1)} %bitcast.5), kind=kLoop, calls=%fused_computation | loop fusion | flops 24576 | bytes 98304 | tf_op jit(solution)/shard_map/stack | solution.py:300
  1.5 5.1 %collective-permute-start = (bf16[2,2,6144]{2,1,0:T(2,128)(2,1)S(1)}, bf16[2,2,6144]{2,1,0:T(2,128)(2,1)S(1)}, u32[]{:S(2)}, u32[]{:S(2)}) collective-permute-start(bf16[2,2,6144]{2,1,0:T(2,128)(2,1)S(1)} %pad_maximum_fusion.refs_3_), channel_id=1, source_target_pairs={{0,12},{1,13},{2,14},{3,15},{4,8},{5,9},{6,10},{7,11},{8,4},{9,5},... | collective-permute-start | bytes 147464 | tf_op jit(solution)/shard_map/ppermute | solution.py:298
  6.6 0.6 collective-permute-start.2
  7.2 0.7 dynamic_slice.3
  7.9 0.9 %collective-permute-done.refs_0_ = bf16[2,2,6144]{2,1,0:T(2,128)(2,1)S(1)} collective-permute-done((bf16[2,2,6144]{2,1,0:T(2,128)(2,1)S(1)}, bf16[2,2,6144]{2,1,0:T(2,128)(2,1)S(1)}, u32[]{:S(2)}, u32[]{:S(2)}) %collective-permute-start) | collective-permute-done | bytes 49184 | tf_op jit(solution)/shard_map/ppermute | solution.py:298
  8.8 2.8 %collective-permute-done.1.refs_1_ = bf16[2,2,6144]{2,1,0:T(2,128)(2,1)S(1)} collective-permute-done((bf16[2,2,6144]{2,1,0:T(2,128)(2,1)S(1)}, bf16[2,2,6144]{2,1,0:T(2,128)(2,1)S(1)}, u32[]{:S(2)}, u32[]{:S(2)}) %collective-permute-start.1) | collective-permute-done | bytes 49184 | tf_op jit(solution)/shard_map/ppermute | solution.py:298
  11.6 0.1 join.2._mine.refs_1_
  11.7 1.6 %collective-permute-start.3 = (bf16[2,8,6144]{2,1,0:T(8,128)(2,1)S(1)}, bf16[2,8,6144]{2,1,0:T(8,128)(2,1)S(1)}, u32[]{:S(2)}, u32[]{:S(2)}) collective-permute-start(bf16[2,8,6144]{2,1,0:T(8,128)(2,1)S(1)} %join.2._mine.refs_1_), channel_id=1, source_target_pairs={{0,2},{1,3},{2,0},{3,1},{4,6},{5,7},{6,4},{7,5},{8,10},{9,11},{10,... | collective-permute-start | bytes 589832 | tf_op jit(solution)/shard_map/ppermute | solution.py:298
  13.3 2.9 %first_tiles.1 = (bf16[2,2,6144,256]{3,2,1,0:T(8,128)(2,1)S(1)}, f32[8,128]{1,0:T(8,128)S(1)}) custom-call(bf16[2,8,6144]{2,1,0:T(8,128)(2,1)S(1)} %join.2._mine.refs_1_, bf16[1,2048]{1,0:T(2,128)(2,1)S(1)} %reshape.25.refs_4_._bias.bias, bf16[6144,2048]{1,0:T(8,128)(2,1)} %weight_hidden.3, bf16[6144,2048]{1,0:T(8,128)(2,1)} %weight_output.3), custom_call_target="tpu_custom_call" | custom-call | bytes 6291456 | tf_op jit(solution)/shard_map/first_tiles/pallas_call | solution.py:70
  16.2 1.4 %collective-permute-done.3.refs_0_ = bf16[2,8,6144]{2,1,0:T(8,128)(2,1)S(1)} collective-permute-done((bf16[2,8,6144]{2,1,0:T(8,128)(2,1)S(1)}, bf16[2,8,6144]{2,1,0:T(8,128)(2,1)S(1)}, u32[]{:S(2)}, u32[]{:S(2)}) %collective-permute-start.3) | collective-permute-done | bytes 196640 | tf_op jit(solution)/shard_map/ppermute | solution.py:298
  17.5 0.1 collective-permute-start.4
  17.6 1.7 %collective-permute-done.4.theirs = bf16[2,16,6144]{2,1,0:T(8,128)(2,1)S(1)} collective-permute-done((bf16[2,16,6144]{2,1,0:T(8,128)(2,1)S(1)}, bf16[2,16,6144]{2,1,0:T(8,128)(2,1)S(1)}, u32[]{:S(2)}, u32[]{:S(2)}) %collective-permute-start.4) | collective-permute-done | bytes 393248 | tf_op jit(solution)/shard_map/ppermute | solution.py:298
  19.3 29.9 %weights_pass.1 = (bf16[32,2048]{1,0:T(8,128)(2,1)S(1)}, bf16[32,2048]{1,0:T(8,128)(2,1)S(1)}, f32[1,2048]{1,0:T(1,128)}, f32[1,6144]{1,0:T(1,128)}, bf16[2,32,6...) custom-call(bf16[2,16,6144]{2,1,0:T(8,128)(2,1)S(1)} %join.3.mine, ...), custom_call_target="tpu_custom_call", output_to_operand_aliasing={{9}: (5, {})} | custom-call | flops 4831838208 | bytes 75497472 | tf_op jit(solution)/shard_map/weights_pass/pallas_call | solution.py:156
  49.2 0.2 collective-permute-start.5
  49.4 2.5 %outer_rows.3 = (bf16[6144,2048]{1,0:T(8,128)(2,1)}, bf16[6144,2048]{1,0:T(8,128)(2,1)}, f32[8,128]{1,0:T(8,128)S(1)}) custom-call(bf16[2,32,6144]{2,1,0:T(8,128)(2,1)S(1)} %get-tuple-element.35.both, bf16[32,2048]{1,0:T(8,128)(2,1)S(1)} %get-tuple-element.36.active, ...), custom_call_target="tpu_custom_call", output_to_operand_aliasing={{0}: (3, {}), {1}: (4, {})} | custom-call | flops 134217728 | bytes 4194304 | tf_op jit(solution)/shard_map/outer_rows/pallas_call | solution.py:214
  52.0 0.1 add_and_split.2
  52.1 1.6 %collective-permute-start.6 = (bf16[2,8,6144]{2,1,0:T(8,128)(2,1)S(1)}, bf16[2,8,6144]{2,1,0:T(8,128)(2,1)S(1)}, u32[]{:S(2)}, u32[]{:S(2)}) collective-permute-start(bf16[2,8,6144]{2,1,0:T(8,128)(2,1)S(1)} %get-tuple-element.47), channel_id=1, source_target_pairs={{0,2},{1,3},{2,0},{3,1},{4,6},{5,7},{6,4},{7,5},{8,10},{9,11},{10,... | collective-permute-start | bytes 589832 | tf_op jit(solution)/shard_map/ppermute | solution.py:298
  53.7 6.8 %outer_rows.4 = (bf16[6144,2048]{1,0:T(8,128)(2,1)}, bf16[6144,2048]{1,0:T(8,128)(2,1)}, f32[8,128]{1,0:T(8,128)S(1)}) custom-call(bf16[2,32,6144]{2,1,0:T(8,128)(2,1)S(1)} %get-tuple-element.35.both, bf16[32,2048]{1,0:T(8,128)(2,1)S(1)} %get-tuple-element.36.active, ...), custom_call_target="tpu_custom_call", output_to_operand_aliasing={{0}: (3, {}), {1}: (4, {})} | custom-call | flops 536870912 | bytes 16777216 | tf_op jit(solution)/shard_map/outer_rows/pallas_call | solution.py:214
  60.4 0.1 add_and_split.3
  60.5 0.8 %collective-permute-start.7 = (bf16[2,2,6144]{2,1,0:T(2,128)(2,1)S(1)}, bf16[2,2,6144]{2,1,0:T(2,128)(2,1)S(1)}, u32[]{:S(2)}, u32[]{:S(2)}) collective-permute-start(bf16[2,2,6144]{2,1,0:T(2,128)(2,1)S(1)} %get-tuple-element.49), channel_id=1, source_target_pairs={{0,4},{1,5},{2,6},{3,7},{4,0},{5,1},{6,2},{7,3},{8,12},{9,13},{10,... | collective-permute-start | bytes 147464 | tf_op jit(solution)/shard_map/ppermute | solution.py:298
  61.3 1.9 %collective-permute-start.8 = (bf16[2,2,6144]{2,1,0:T(2,128)(2,1)S(1)}, bf16[2,2,6144]{2,1,0:T(2,128)(2,1)S(1)}, u32[]{:S(2)}, u32[]{:S(2)}) collective-permute-start(bf16[2,2,6144]{2,1,0:T(2,128)(2,1)S(1)} %get-tuple-element.50), channel_id=1, source_target_pairs={{0,8},{1,9},{2,10},{3,11},{4,12},{5,13},{6,14},{7,15},{8,0},{9,1},... | collective-permute-start | bytes 147464 | tf_op jit(solution)/shard_map/ppermute | solution.py:298
  63.2 1.8 %collective-permute-start.9 = (bf16[2,2,6144]{2,1,0:T(2,128)(2,1)S(1)}, bf16[2,2,6144]{2,1,0:T(2,128)(2,1)S(1)}, u32[]{:S(2)}, u32[]{:S(2)}) collective-permute-start(bf16[2,2,6144]{2,1,0:T(2,128)(2,1)S(1)} %get-tuple-element.51), channel_id=1, source_target_pairs={{0,12},{1,13},{2,14},{3,15},{4,8},{5,9},{6,10},{7,11},{8,4},{9,5},... | collective-permute-start | bytes 147464 | tf_op jit(solution)/shard_map/ppermute | solution.py:298
  65.0 6.7 %outer_rows.5 = (bf16[6144,2048]{1,0:T(8,128)(2,1)}, bf16[6144,2048]{1,0:T(8,128)(2,1)}, f32[8,128]{1,0:T(8,128)}) custom-call(bf16[2,32,6144]{2,1,0:T(8,128)(2,1)S(1)} %get-tuple-element.35.both, bf16[32,2048]{1,0:T(8,128)(2,1)S(1)} %get-tuple-element.36.active, ...), custom_call_target="tpu_custom_call", output_to_operand_aliasing={{0}: (3, {}), {1}: (4, {})} | custom-call | flops 536870912 | bytes 16777216 | tf_op jit(solution)/shard_map/outer_rows/pallas_call | solution.py:214
  71.7 0.7 last_sum.1
  (12 shorter events, 0.1 us)
Async XLA Ops:
  1.5 7.3 %collective-permute-start = (bf16[2,2,6144]{2,1,0:T(2,128)(2,1)S(1)}, bf16[2,2,6144]{2,1,0:T(2,128)(2,1)S(1)}, u32[]{:S(2)}, u32[]{:S(2)}) collective-permute-start(bf16[2,2,6144]{2,1,0:T(2,128)(2,1)S(1)} %pad_maximum_fusion.refs_3_), channel_id=1, source_target_pairs={{0,12},{1,13},{2,14},{3,15},{4,8},{5,9},{6,10},{7,11},{8,4},{9,5},... | collective-permute-start | bytes 147464 | tf_op jit(solution)/shard_map/ppermute | solution.py:298
  6.6 5.0 %collective-permute-start.1 = (bf16[2,2,6144]{2,1,0:T(2,128)(2,1)S(1)}, bf16[2,2,6144]{2,1,0:T(2,128)(2,1)S(1)}, u32[]{:S(2)}, u32[]{:S(2)}) collective-permute-start(bf16[2,2,6144]{2,1,0:T(2,128)(2,1)S(1)} %pad_maximum_fusion.refs_3_), channel_id=1, source_target_pairs={{0,8},{1,9},{2,10},{3,11},{4,12},{5,13},{6,14},{7,15},{8,0},{9,1},... | collective-permute-start | bytes 147464 | tf_op jit(solution)/shard_map/ppermute | solution.py:298
  6.6 5.0 %collective-permute-start.2 = (bf16[2,2,6144]{2,1,0:T(2,128)(2,1)S(1)}, bf16[2,2,6144]{2,1,0:T(2,128)(2,1)S(1)}, u32[]{:S(2)}, u32[]{:S(2)}) collective-permute-start(bf16[2,2,6144]{2,1,0:T(2,128)(2,1)S(1)} %pad_maximum_fusion.refs_3_), channel_id=1, source_target_pairs={{0,4},{1,5},{2,6},{3,7},{4,0},{5,1},{6,2},{7,3},{8,12},{9,13},{10,... | collective-permute-start | bytes 147464 | tf_op jit(solution)/shard_map/ppermute | solution.py:298
  11.7 5.8 %collective-permute-start.3 = (bf16[2,8,6144]{2,1,0:T(8,128)(2,1)S(1)}, bf16[2,8,6144]{2,1,0:T(8,128)(2,1)S(1)}, u32[]{:S(2)}, u32[]{:S(2)}) collective-permute-start(bf16[2,8,6144]{2,1,0:T(8,128)(2,1)S(1)} %join.2._mine.refs_1_), channel_id=1, source_target_pairs={{0,2},{1,3},{2,0},{3,1},{4,6},{5,7},{6,4},{7,5},{8,10},{9,11},{10,... | collective-permute-start | bytes 589832 | tf_op jit(solution)/shard_map/ppermute | solution.py:298
  17.5 1.8 %collective-permute-start.4 = (bf16[2,16,6144]{2,1,0:T(8,128)(2,1)S(1)}, bf16[2,16,6144]{2,1,0:T(8,128)(2,1)S(1)}, u32[]{:S(2)}, u32[]{:S(2)}) collective-permute-start(bf16[2,16,6144]{2,1,0:T(8,128)(2,1)S(1)} %join.3.mine), channel_id=1, source_target_pairs={{0,1},{1,0},{2,3},{3,2},{4,5},{5,4},{6,7},{7,6},{8,9},{9,8},{10,11... | collective-permute-start | bytes 1179656 | tf_op jit(solution)/shard_map/ppermute | solution.py:298
  49.2 2.7 %collective-permute-start.5 = (f32[2,16,6144]{2,1,0:T(8,128)S(1)}, f32[2,16,6144]{2,1,0:T(8,128)S(1)}, u32[]{:S(2)}, u32[]{:S(2)}) collective-permute-start(f32[2,16,6144]{2,1,0:T(8,128)S(1)} %get-tuple-element.45), channel_id=1, source_target_pairs={{0,1},{1,0},{2,3},{3,2},{4,5},{5,4},{6,7},{7,6},{8,9},{9,8},{10,11... | collective-permute-start | bytes 2359304 | tf_op jit(solution)/shard_map/ppermute | solution.py:298
  49.4 4.2 %copy-start = (bf16[6144]{0:T(1024)(128)(2,1)S(1)}, bf16[6144]{0:T(1024)(128)(2,1)}, u32[]{:S(2)}) copy-start(bf16[6144]{0:T(1024)(128)(2,1)} %param.10) | copy-start | bytes 36868
  52.1 8.4 %collective-permute-start.6 = (bf16[2,8,6144]{2,1,0:T(8,128)(2,1)S(1)}, bf16[2,8,6144]{2,1,0:T(8,128)(2,1)S(1)}, u32[]{:S(2)}, u32[]{:S(2)}) collective-permute-start(bf16[2,8,6144]{2,1,0:T(8,128)(2,1)S(1)} %get-tuple-element.47), channel_id=1, source_target_pairs={{0,2},{1,3},{2,0},{3,1},{4,6},{5,7},{6,4},{7,5},{8,10},{9,11},{10,... | collective-permute-start | bytes 589832 | tf_op jit(solution)/shard_map/ppermute | solution.py:298
  60.5 11.2 %collective-permute-start.7 = (bf16[2,2,6144]{2,1,0:T(2,128)(2,1)S(1)}, bf16[2,2,6144]{2,1,0:T(2,128)(2,1)S(1)}, u32[]{:S(2)}, u32[]{:S(2)}) collective-permute-start(bf16[2,2,6144]{2,1,0:T(2,128)(2,1)S(1)} %get-tuple-element.49), channel_id=1, source_target_pairs={{0,4},{1,5},{2,6},{3,7},{4,0},{5,1},{6,2},{7,3},{8,12},{9,13},{10,... | collective-permute-start | bytes 147464 | tf_op jit(solution)/shard_map/ppermute | solution.py:298
  61.3 10.4 %collective-permute-start.8 = (bf16[2,2,6144]{2,1,0:T(2,128)(2,1)S(1)}, bf16[2,2,6144]{2,1,0:T(2,128)(2,1)S(1)}, u32[]{:S(2)}, u32[]{:S(2)}) collective-permute-start(bf16[2,2,6144]{2,1,0:T(2,128)(2,1)S(1)} %get-tuple-element.50), channel_id=1, source_target_pairs={{0,8},{1,9},{2,10},{3,11},{4,12},{5,13},{6,14},{7,15},{8,0},{9,1},... | collective-permute-start | bytes 147464 | tf_op jit(solution)/shard_map/ppermute | solution.py:298
  63.2 8.6 %collective-permute-start.9 = (bf16[2,2,6144]{2,1,0:T(2,128)(2,1)S(1)}, bf16[2,2,6144]{2,1,0:T(2,128)(2,1)S(1)}, u32[]{:S(2)}, u32[]{:S(2)}) collective-permute-start(bf16[2,2,6144]{2,1,0:T(2,128)(2,1)S(1)} %get-tuple-element.51), channel_id=1, source_target_pairs={{0,12},{1,13},{2,14},{3,15},{4,8},{5,9},{6,10},{7,11},{8,4},{9,5},... | collective-permute-start | bytes 147464 | tf_op jit(solution)/shard_map/ppermute | solution.py:298

commit v4 on v3

--- a/solution.py
+++ b/solution.py
@@ -131,20 +131,21 @@
     weight_output = slots[slot, 1]
     place = pl.ds(pl.multiple_of(step * tile, tile), tile)
     hidden = product(both[0], weight_hidden, ((1,), (0,))) + bias[:, place].astype(F32)
+    grad_active = product(both[1], weight_output, ((1,), (0,)))
     value, slope = gelu_and_slope(hidden)
     value = value.astype(BF16)
     active[:, place] = value
-    grad = (product(both[1], weight_output, ((1,), (0,))) * slope).astype(BF16)
+    grad = (grad_active * slope).astype(BF16)
     grad_hidden[:, place] = grad
     grad_bias_hidden[...] = jnp.sum(grad.astype(F32), axis=0, keepdims=True)
     share = product(value, weight_output, ((1,), (1,)))
     keep[0] += share[:near]
     send[0] += share[near:]
+    grad_weight_output[...] = product(turned[1], value, ((1,), (0,))).astype(BF16)
     share = product(grad, weight_hidden, ((1,), (1,)))
     keep[1] += share[:near]
     send[1] += share[near:]
     grad_weight_hidden[...] = product(turned[0], grad, ((1,), (0,))).astype(BF16)
-    grad_weight_output[...] = product(turned[1], value, ((1,), (0,))).astype(BF16)
 
 
 def weights_pass(mine, theirs, bias, weight_hidden, weight_output, slots, rows):

time: 72.7 us -> 72.1 us (level)
  no operation moved by 1% of the time
where the time goes in v4:
time: 72.1 us; the launch traced here: 71.9 us
  Pallas kernels  49.3 us (68%)
  starting transfers between devices  13.6 us (19%)
  waiting for transfers between devices  6.73 us (9%)
  other arithmetic  0.83 us (1%)
    pallas_call x1, Pallas kernels, weights_pass(): pl.pallas_call(weights_body, grid=(units // tile,), in_specs=[HELD, HELD,...  29.3 us
    pallas_call x3, Pallas kernels, outer_rows(): pl.pallas_call(functools.partial(outer_body, first), grid=(steps,), in_sp...  16 us
    ppermute x10, starting transfers between devices, swap(): return lax.ppermute(value, 'gx', [(i, i ^ step) for i in range(devices)])  13.6 us
    ppermute x10, waiting for transfers between devices, swap(): return lax.ppermute(value, 'gx', [(i, i ^ step) for i in range(devices)])  6.73 us
    pallas_call x1, Pallas kernels, first_tiles(): pl.pallas_call(first_body, in_specs=[HELD, HELD, FAR, FAR], out_specs=[HE...  2.89 us
  transfers between devices with their start and end apart: 10, of which 4 were waited for; matrix products, arithmetic and copies ran while one was open for 1% of the time, Pallas kernels for 26%

profile of v4, /device:TPU:0, one launch (start us, length us, event | category | flops | bytes accessed | tf_op | source)
XLA Modules:
  0.0 71.9 jit_solution(2946089183823812629)
XLA Ops:
  0.6 0.8 %pad_maximum_fusion.refs_3_ = bf16[2,2,6144]{2,1,0:T(2,128)(2,1)S(1)} fusion(bf16[1,2,6144]{2,1,0:T(2,128)(2,1)} %bitcast.4, bf16[1,2,6144]{2,1,0:T(2,128)(2,1)} %bitcast.5), kind=kLoop, calls=%fused_computation | loop fusion | flops 24576 | bytes 98304 | tf_op jit(solution)/shard_map/stack | solution.py:301
  1.5 5.1 %collective-permute-start = (bf16[2,2,6144]{2,1,0:T(2,128)(2,1)S(1)}, bf16[2,2,6144]{2,1,0:T(2,128)(2,1)S(1)}, u32[]{:S(2)}, u32[]{:S(2)}) collective-permute-start(bf16[2,2,6144]{2,1,0:T(2,128)(2,1)S(1)} %pad_maximum_fusion.refs_3_), channel_id=1, source_target_pairs={{0,12},{1,13},{2,14},{3,15},{4,8},{5,9},{6,10},{7,11},{8,4},{9,5},... | collective-permute-start | bytes 147464 | tf_op jit(solution)/shard_map/ppermute | solution.py:299
  6.6 0.6 collective-permute-start.2
  7.2 0.7 dynamic_slice.3
  7.9 0.9 %collective-permute-done.refs_0_ = bf16[2,2,6144]{2,1,0:T(2,128)(2,1)S(1)} collective-permute-done((bf16[2,2,6144]{2,1,0:T(2,128)(2,1)S(1)}, bf16[2,2,6144]{2,1,0:T(2,128)(2,1)S(1)}, u32[]{:S(2)}, u32[]{:S(2)}) %collective-permute-start) | collective-permute-done | bytes 49184 | tf_op jit(solution)/shard_map/ppermute | solution.py:299
  8.8 2.8 %collective-permute-done.1.refs_1_ = bf16[2,2,6144]{2,1,0:T(2,128)(2,1)S(1)} collective-permute-done((bf16[2,2,6144]{2,1,0:T(2,128)(2,1)S(1)}, bf16[2,2,6144]{2,1,0:T(2,128)(2,1)S(1)}, u32[]{:S(2)}, u32[]{:S(2)}) %collective-permute-start.1) | collective-permute-done | bytes 49184 | tf_op jit(solution)/shard_map/ppermute | solution.py:299
  11.6 0.1 join.2._mine.refs_1_
  11.7 1.6 %collective-permute-start.3 = (bf16[2,8,6144]{2,1,0:T(8,128)(2,1)S(1)}, bf16[2,8,6144]{2,1,0:T(8,128)(2,1)S(1)}, u32[]{:S(2)}, u32[]{:S(2)}) collective-permute-start(bf16[2,8,6144]{2,1,0:T(8,128)(2,1)S(1)} %join.2._mine.refs_1_), channel_id=1, source_target_pairs={{0,2},{1,3},{2,0},{3,1},{4,6},{5,7},{6,4},{7,5},{8,10},{9,11},{10,... | collective-permute-start | bytes 589832 | tf_op jit(solution)/shard_map/ppermute | solution.py:299
  13.3 2.9 %first_tiles.1 = (bf16[2,2,6144,256]{3,2,1,0:T(8,128)(2,1)S(1)}, f32[8,128]{1,0:T(8,128)S(1)}) custom-call(bf16[2,8,6144]{2,1,0:T(8,128)(2,1)S(1)} %join.2._mine.refs_1_, bf16[1,2048]{1,0:T(2,128)(2,1)S(1)} %reshape.25.refs_4_._bias.bias, bf16[6144,2048]{1,0:T(8,128)(2,1)} %weight_hidden.3, bf16[6144,2048]{1,0:T(8,128)(2,1)} %weight_output.3), custom_call_target="tpu_custom_call" | custom-call | bytes 6291456 | tf_op jit(solution)/shard_map/first_tiles/pallas_call | solution.py:70
  16.2 1.4 %collective-permute-done.3.refs_0_ = bf16[2,8,6144]{2,1,0:T(8,128)(2,1)S(1)} collective-permute-done((bf16[2,8,6144]{2,1,0:T(8,128)(2,1)S(1)}, bf16[2,8,6144]{2,1,0:T(8,128)(2,1)S(1)}, u32[]{:S(2)}, u32[]{:S(2)}) %collective-permute-start.3) | collective-permute-done | bytes 196640 | tf_op jit(solution)/shard_map/ppermute | solution.py:299
  17.5 0.1 collective-permute-start.4
  17.6 1.7 %collective-permute-done.4.theirs = bf16[2,16,6144]{2,1,0:T(8,128)(2,1)S(1)} collective-permute-done((bf16[2,16,6144]{2,1,0:T(8,128)(2,1)S(1)}, bf16[2,16,6144]{2,1,0:T(8,128)(2,1)S(1)}, u32[]{:S(2)}, u32[]{:S(2)}) %collective-permute-start.4) | collective-permute-done | bytes 393248 | tf_op jit(solution)/shard_map/ppermute | solution.py:299
  19.3 29.3 %weights_pass.1 = (bf16[32,2048]{1,0:T(8,128)(2,1)S(1)}, bf16[32,2048]{1,0:T(8,128)(2,1)S(1)}, f32[1,2048]{1,0:T(1,128)}, f32[1,6144]{1,0:T(1,128)}, bf16[2,32,6...) custom-call(bf16[2,16,6144]{2,1,0:T(8,128)(2,1)S(1)} %join.3.mine, ...), custom_call_target="tpu_custom_call", output_to_operand_aliasing={{9}: (5, {})} | custom-call | flops 4831838208 | bytes 75497472 | tf_op jit(solution)/shard_map/weights_pass/pallas_call | solution.py:157
  48.7 0.2 collective-permute-start.5
  48.9 2.5 %outer_rows.3 = (bf16[6144,2048]{1,0:T(8,128)(2,1)}, bf16[6144,2048]{1,0:T(8,128)(2,1)}, f32[8,128]{1,0:T(8,128)S(1)}) custom-call(bf16[2,32,6144]{2,1,0:T(8,128)(2,1)S(1)} %get-tuple-element.35.both, bf16[32,2048]{1,0:T(8,128)(2,1)S(1)} %get-tuple-element.36.active, ...), custom_call_target="tpu_custom_call", output_to_operand_aliasing={{0}: (3, {}), {1}: (4, {})} | custom-call | flops 134217728 | bytes 4194304 | tf_op jit(solution)/shard_map/outer_rows/pallas_call | solution.py:215
  51.4 0.1 add_and_split.2
  51.5 1.6 %collective-permute-start.6 = (bf16[2,8,6144]{2,1,0:T(8,128)(2,1)S(1)}, bf16[2,8,6144]{2,1,0:T(8,128)(2,1)S(1)}, u32[]{:S(2)}, u32[]{:S(2)}) collective-permute-start(bf16[2,8,6144]{2,1,0:T(8,128)(2,1)S(1)} %get-tuple-element.47), channel_id=1, source_target_pairs={{0,2},{1,3},{2,0},{3,1},{4,6},{5,7},{6,4},{7,5},{8,10},{9,11},{10,... | collective-permute-start | bytes 589832 | tf_op jit(solution)/shard_map/ppermute | solution.py:299
  53.1 6.8 %outer_rows.4 = (bf16[6144,2048]{1,0:T(8,128)(2,1)}, bf16[6144,2048]{1,0:T(8,128)(2,1)}, f32[8,128]{1,0:T(8,128)S(1)}) custom-call(bf16[2,32,6144]{2,1,0:T(8,128)(2,1)S(1)} %get-tuple-element.35.both, bf16[32,2048]{1,0:T(8,128)(2,1)S(1)} %get-tuple-element.36.active, ...), custom_call_target="tpu_custom_call", output_to_operand_aliasing={{0}: (3, {}), {1}: (4, {})} | custom-call | flops 536870912 | bytes 16777216 | tf_op jit(solution)/shard_map/outer_rows/pallas_call | solution.py:215
  59.9 0.1 add_and_split.3
  60.0 0.8 %collective-permute-start.7 = (bf16[2,2,6144]{2,1,0:T(2,128)(2,1)S(1)}, bf16[2,2,6144]{2,1,0:T(2,128)(2,1)S(1)}, u32[]{:S(2)}, u32[]{:S(2)}) collective-permute-start(bf16[2,2,6144]{2,1,0:T(2,128)(2,1)S(1)} %get-tuple-element.49), channel_id=1, source_target_pairs={{0,4},{1,5},{2,6},{3,7},{4,0},{5,1},{6,2},{7,3},{8,12},{9,13},{10,... | collective-permute-start | bytes 147464 | tf_op jit(solution)/shard_map/ppermute | solution.py:299
  60.8 1.9 %collective-permute-start.8 = (bf16[2,2,6144]{2,1,0:T(2,128)(2,1)S(1)}, bf16[2,2,6144]{2,1,0:T(2,128)(2,1)S(1)}, u32[]{:S(2)}, u32[]{:S(2)}) collective-permute-start(bf16[2,2,6144]{2,1,0:T(2,128)(2,1)S(1)} %get-tuple-element.50), channel_id=1, source_target_pairs={{0,8},{1,9},{2,10},{3,11},{4,12},{5,13},{6,14},{7,15},{8,0},{9,1},... | collective-permute-start | bytes 147464 | tf_op jit(solution)/shard_map/ppermute | solution.py:299
  62.6 1.8 %collective-permute-start.9 = (bf16[2,2,6144]{2,1,0:T(2,128)(2,1)S(1)}, bf16[2,2,6144]{2,1,0:T(2,128)(2,1)S(1)}, u32[]{:S(2)}, u32[]{:S(2)}) collective-permute-start(bf16[2,2,6144]{2,1,0:T(2,128)(2,1)S(1)} %get-tuple-element.51), channel_id=1, source_target_pairs={{0,12},{1,13},{2,14},{3,15},{4,8},{5,9},{6,10},{7,11},{8,4},{9,5},... | collective-permute-start | bytes 147464 | tf_op jit(solution)/shard_map/ppermute | solution.py:299
  64.4 6.7 %outer_rows.5 = (bf16[6144,2048]{1,0:T(8,128)(2,1)}, bf16[6144,2048]{1,0:T(8,128)(2,1)}, f32[8,128]{1,0:T(8,128)}) custom-call(bf16[2,32,6144]{2,1,0:T(8,128)(2,1)S(1)} %get-tuple-element.35.both, bf16[32,2048]{1,0:T(8,128)(2,1)S(1)} %get-tuple-element.36.active, ...), custom_call_target="tpu_custom_call", output_to_operand_aliasing={{0}: (3, {}), {1}: (4, {})} | custom-call | flops 536870912 | bytes 16777216 | tf_op jit(solution)/shard_map/outer_rows/pallas_call | solution.py:215
  71.2 0.7 last_sum.1
  (12 shorter events, 0.1 us)
Async XLA Ops:
  1.5 7.3 %collective-permute-start = (bf16[2,2,6144]{2,1,0:T(2,128)(2,1)S(1)}, bf16[2,2,6144]{2,1,0:T(2,128)(2,1)S(1)}, u32[]{:S(2)}, u32[]{:S(2)}) collective-permute-start(bf16[2,2,6144]{2,1,0:T(2,128)(2,1)S(1)} %pad_maximum_fusion.refs_3_), channel_id=1, source_target_pairs={{0,12},{1,13},{2,14},{3,15},{4,8},{5,9},{6,10},{7,11},{8,4},{9,5},... | collective-permute-start | bytes 147464 | tf_op jit(solution)/shard_map/ppermute | solution.py:299
  6.6 5.0 %collective-permute-start.1 = (bf16[2,2,6144]{2,1,0:T(2,128)(2,1)S(1)}, bf16[2,2,6144]{2,1,0:T(2,128)(2,1)S(1)}, u32[]{:S(2)}, u32[]{:S(2)}) collective-permute-start(bf16[2,2,6144]{2,1,0:T(2,128)(2,1)S(1)} %pad_maximum_fusion.refs_3_), channel_id=1, source_target_pairs={{0,8},{1,9},{2,10},{3,11},{4,12},{5,13},{6,14},{7,15},{8,0},{9,1},... | collective-permute-start | bytes 147464 | tf_op jit(solution)/shard_map/ppermute | solution.py:299
  6.6 5.0 %collective-permute-start.2 = (bf16[2,2,6144]{2,1,0:T(2,128)(2,1)S(1)}, bf16[2,2,6144]{2,1,0:T(2,128)(2,1)S(1)}, u32[]{:S(2)}, u32[]{:S(2)}) collective-permute-start(bf16[2,2,6144]{2,1,0:T(2,128)(2,1)S(1)} %pad_maximum_fusion.refs_3_), channel_id=1, source_target_pairs={{0,4},{1,5},{2,6},{3,7},{4,0},{5,1},{6,2},{7,3},{8,12},{9,13},{10,... | collective-permute-start | bytes 147464 | tf_op jit(solution)/shard_map/ppermute | solution.py:299
  11.7 5.8 %collective-permute-start.3 = (bf16[2,8,6144]{2,1,0:T(8,128)(2,1)S(1)}, bf16[2,8,6144]{2,1,0:T(8,128)(2,1)S(1)}, u32[]{:S(2)}, u32[]{:S(2)}) collective-permute-start(bf16[2,8,6144]{2,1,0:T(8,128)(2,1)S(1)} %join.2._mine.refs_1_), channel_id=1, source_target_pairs={{0,2},{1,3},{2,0},{3,1},{4,6},{5,7},{6,4},{7,5},{8,10},{9,11},{10,... | collective-permute-start | bytes 589832 | tf_op jit(solution)/shard_map/ppermute | solution.py:299
  17.5 1.8 %collective-permute-start.4 = (bf16[2,16,6144]{2,1,0:T(8,128)(2,1)S(1)}, bf16[2,16,6144]{2,1,0:T(8,128)(2,1)S(1)}, u32[]{:S(2)}, u32[]{:S(2)}) collective-permute-start(bf16[2,16,6144]{2,1,0:T(8,128)(2,1)S(1)} %join.3.mine), channel_id=1, source_target_pairs={{0,1},{1,0},{2,3},{3,2},{4,5},{5,4},{6,7},{7,6},{8,9},{9,8},{10,11... | collective-permute-start | bytes 1179656 | tf_op jit(solution)/shard_map/ppermute | solution.py:299
  48.7 2.7 %collective-permute-start.5 = (f32[2,16,6144]{2,1,0:T(8,128)S(1)}, f32[2,16,6144]{2,1,0:T(8,128)S(1)}, u32[]{:S(2)}, u32[]{:S(2)}) collective-permute-start(f32[2,16,6144]{2,1,0:T(8,128)S(1)} %get-tuple-element.45), channel_id=1, source_target_pairs={{0,1},{1,0},{2,3},{3,2},{4,5},{5,4},{6,7},{7,6},{8,9},{9,8},{10,11... | collective-permute-start | bytes 2359304 | tf_op jit(solution)/shard_map/ppermute | solution.py:299
  48.9 4.2 %copy-start = (bf16[6144]{0:T(1024)(128)(2,1)S(1)}, bf16[6144]{0:T(1024)(128)(2,1)}, u32[]{:S(2)}) copy-start(bf16[6144]{0:T(1024)(128)(2,1)} %param.10) | copy-start | bytes 36868
  51.5 8.4 %collective-permute-start.6 = (bf16[2,8,6144]{2,1,0:T(8,128)(2,1)S(1)}, bf16[2,8,6144]{2,1,0:T(8,128)(2,1)S(1)}, u32[]{:S(2)}, u32[]{:S(2)}) collective-permute-start(bf16[2,8,6144]{2,1,0:T(8,128)(2,1)S(1)} %get-tuple-element.47), channel_id=1, source_target_pairs={{0,2},{1,3},{2,0},{3,1},{4,6},{5,7},{6,4},{7,5},{8,10},{9,11},{10,... | collective-permute-start | bytes 589832 | tf_op jit(solution)/shard_map/ppermute | solution.py:299
  60.0 11.2 %collective-permute-start.7 = (bf16[2,2,6144]{2,1,0:T(2,128)(2,1)S(1)}, bf16[2,2,6144]{2,1,0:T(2,128)(2,1)S(1)}, u32[]{:S(2)}, u32[]{:S(2)}) collective-permute-start(bf16[2,2,6144]{2,1,0:T(2,128)(2,1)S(1)} %get-tuple-element.49), channel_id=1, source_target_pairs={{0,4},{1,5},{2,6},{3,7},{4,0},{5,1},{6,2},{7,3},{8,12},{9,13},{10,... | collective-permute-start | bytes 147464 | tf_op jit(solution)/shard_map/ppermute | solution.py:299
  60.8 10.4 %collective-permute-start.8 = (bf16[2,2,6144]{2,1,0:T(2,128)(2,1)S(1)}, bf16[2,2,6144]{2,1,0:T(2,128)(2,1)S(1)}, u32[]{:S(2)}, u32[]{:S(2)}) collective-permute-start(bf16[2,2,6144]{2,1,0:T(2,128)(2,1)S(1)} %get-tuple-element.50), channel_id=1, source_target_pairs={{0,8},{1,9},{2,10},{3,11},{4,12},{5,13},{6,14},{7,15},{8,0},{9,1},... | collective-permute-start | bytes 147464 | tf_op jit(solution)/shard_map/ppermute | solution.py:299
  62.6 8.6 %collective-permute-start.9 = (bf16[2,2,6144]{2,1,0:T(2,128)(2,1)S(1)}, bf16[2,2,6144]{2,1,0:T(2,128)(2,1)S(1)}, u32[]{:S(2)}, u32[]{:S(2)}) collective-permute-start(bf16[2,2,6144]{2,1,0:T(2,128)(2,1)S(1)} %get-tuple-element.51), channel_id=1, source_target_pairs={{0,12},{1,13},{2,14},{3,15},{4,8},{5,9},{6,10},{7,11},{8,4},{9,5},... | collective-permute-start | bytes 147464 | tf_op jit(solution)/shard_map/ppermute | solution.py:299

commit v5 on v4

--- a/solution.py
+++ b/solution.py
@@ -14,7 +14,7 @@
 CUBE = 0.044715
 VMEM = 24 * 2**20
 STEPS = 24
-PASS = 6
+PASS = 8
 CORE = 2
 HOP = 8
 HELD = pl.BlockSpec(memory_space=pltpu.VMEM)
@@ -312,7 +312,8 @@
 
     part = width // STEPS
     done = PASS
-    beside = [CORE] + [HOP] * (len(levels) - 2)
+    hop = HOP if len(levels) <= 3 else (STEPS - done - CORE) // (len(levels) - 1)
+    beside = [CORE] + [hop] * (len(levels) - 2)
     beside.append(STEPS - done - sum(beside))
     (active, grad_hidden, grad_bias_hidden, grad_bias_output, both, keep, send, grad_weight_hidden,
      grad_weight_output, _) = weights_pass(

time: 72.1 us -> 72.1 us (level)
    pallas_call x3, Pallas kernels: 16 us -> 14.7 us  [outer_rows(): pl.pallas_call(functools.partial(outer_body, first), grid=(steps,), in_sp...]
    pallas_call x1, Pallas kernels: 29.3 us -> 30.6 us  [weights_pass(): pl.pallas_call(weights_body, grid=(units // tile,), in_specs=[HELD, HELD,...]
  transfers between devices with their start and end apart: 10 -> 10, of which waited for: 4 -> 4; matrix products, arithmetic and copies ran while one was open for 1% -> 1% of each run, Pallas kernels for 26% -> 24%
where the time goes in v5:
time: 72.1 us; the launch traced here: 71.9 us
  Pallas kernels  49.3 us (68%)
  starting transfers between devices  13.6 us (19%)
  waiting for transfers between devices  6.73 us (9%)
  other arithmetic  0.83 us (1%)
    pallas_call x1, Pallas kernels, weights_pass(): pl.pallas_call(weights_body, grid=(units // tile,), in_specs=[HELD, HELD,...  30.6 us
    pallas_call x3, Pallas kernels, outer_rows(): pl.pallas_call(functools.partial(outer_body, first), grid=(steps,), in_sp...  14.7 us
    ppermute x10, starting transfers between devices, swap(): return lax.ppermute(value, 'gx', [(i, i ^ step) for i in range(devices)])  13.6 us
    ppermute x10, waiting for transfers between devices, swap(): return lax.ppermute(value, 'gx', [(i, i ^ step) for i in range(devices)])  6.73 us
    pallas_call x1, Pallas kernels, first_tiles(): pl.pallas_call(first_body, in_specs=[HELD, HELD, FAR, FAR], out_specs=[HE...  2.89 us
  transfers between devices with their start and end apart: 10, of which 4 were waited for; matrix products, arithmetic and copies ran while one was open for 1% of the time, Pallas kernels for 24%

profile of v5, /device:TPU:0, one launch (start us, length us, event | category | flops | bytes accessed | tf_op | source)
XLA Modules:
  0.0 71.9 jit_solution(9453014056946578913)
XLA Ops:
  0.6 0.8 %pad_maximum_fusion.refs_3_ = bf16[2,2,6144]{2,1,0:T(2,128)(2,1)S(1)} fusion(bf16[1,2,6144]{2,1,0:T(2,128)(2,1)} %bitcast.4, bf16[1,2,6144]{2,1,0:T(2,128)(2,1)} %bitcast.5), kind=kLoop, calls=%fused_computation | loop fusion | flops 24576 | bytes 98304 | tf_op jit(solution)/shard_map/stack | solution.py:301
  1.5 5.1 %collective-permute-start = (bf16[2,2,6144]{2,1,0:T(2,128)(2,1)S(1)}, bf16[2,2,6144]{2,1,0:T(2,128)(2,1)S(1)}, u32[]{:S(2)}, u32[]{:S(2)}) collective-permute-start(bf16[2,2,6144]{2,1,0:T(2,128)(2,1)S(1)} %pad_maximum_fusion.refs_3_), channel_id=1, source_target_pairs={{0,12},{1,13},{2,14},{3,15},{4,8},{5,9},{6,10},{7,11},{8,4},{9,5},... | collective-permute-start | bytes 147464 | tf_op jit(solution)/shard_map/ppermute | solution.py:299
  6.6 0.6 collective-permute-start.2
  7.2 0.7 dynamic_slice.3
  7.9 0.9 %collective-permute-done.refs_0_ = bf16[2,2,6144]{2,1,0:T(2,128)(2,1)S(1)} collective-permute-done((bf16[2,2,6144]{2,1,0:T(2,128)(2,1)S(1)}, bf16[2,2,6144]{2,1,0:T(2,128)(2,1)S(1)}, u32[]{:S(2)}, u32[]{:S(2)}) %collective-permute-start) | collective-permute-done | bytes 49184 | tf_op jit(solution)/shard_map/ppermute | solution.py:299
  8.8 2.8 %collective-permute-done.1.refs_1_ = bf16[2,2,6144]{2,1,0:T(2,128)(2,1)S(1)} collective-permute-done((bf16[2,2,6144]{2,1,0:T(2,128)(2,1)S(1)}, bf16[2,2,6144]{2,1,0:T(2,128)(2,1)S(1)}, u32[]{:S(2)}, u32[]{:S(2)}) %collective-permute-start.1) | collective-permute-done | bytes 49184 | tf_op jit(solution)/shard_map/ppermute | solution.py:299
  11.6 0.1 join.2._mine.refs_1_
  11.7 1.6 %collective-permute-start.3 = (bf16[2,8,6144]{2,1,0:T(8,128)(2,1)S(1)}, bf16[2,8,6144]{2,1,0:T(8,128)(2,1)S(1)}, u32[]{:S(2)}, u32[]{:S(2)}) collective-permute-start(bf16[2,8,6144]{2,1,0:T(8,128)(2,1)S(1)} %join.2._mine.refs_1_), channel_id=1, source_target_pairs={{0,2},{1,3},{2,0},{3,1},{4,6},{5,7},{6,4},{7,5},{8,10},{9,11},{10,... | collective-permute-start | bytes 589832 | tf_op jit(solution)/shard_map/ppermute | solution.py:299
  13.3 2.9 %first_tiles.1 = (bf16[2,2,6144,256]{3,2,1,0:T(8,128)(2,1)S(1)}, f32[8,128]{1,0:T(8,128)S(1)}) custom-call(bf16[2,8,6144]{2,1,0:T(8,128)(2,1)S(1)} %join.2._mine.refs_1_, bf16[1,2048]{1,0:T(2,128)(2,1)S(1)} %reshape.25.refs_4_._bias.bias, bf16[6144,2048]{1,0:T(8,128)(2,1)} %weight_hidden.3, bf16[6144,2048]{1,0:T(8,128)(2,1)} %weight_output.3), custom_call_target="tpu_custom_call" | custom-call | bytes 6291456 | tf_op jit(solution)/shard_map/first_tiles/pallas_call | solution.py:70
  16.2 1.4 %collective-permute-done.3.refs_0_ = bf16[2,8,6144]{2,1,0:T(8,128)(2,1)S(1)} collective-permute-done((bf16[2,8,6144]{2,1,0:T(8,128)(2,1)S(1)}, bf16[2,8,6144]{2,1,0:T(8,128)(2,1)S(1)}, u32[]{:S(2)}, u32[]{:S(2)}) %collective-permute-start.3) | collective-permute-done | bytes 196640 | tf_op jit(solution)/shard_map/ppermute | solution.py:299
  17.5 0.1 collective-permute-start.4
  17.6 1.7 %collective-permute-done.4.theirs = bf16[2,16,6144]{2,1,0:T(8,128)(2,1)S(1)} collective-permute-done((bf16[2,16,6144]{2,1,0:T(8,128)(2,1)S(1)}, bf16[2,16,6144]{2,1,0:T(8,128)(2,1)S(1)}, u32[]{:S(2)}, u32[]{:S(2)}) %collective-permute-start.4) | collective-permute-done | bytes 393248 | tf_op jit(solution)/shard_map/ppermute | solution.py:299
  19.3 30.6 %weights_pass.1 = (bf16[32,2048]{1,0:T(8,128)(2,1)S(1)}, bf16[32,2048]{1,0:T(8,128)(2,1)S(1)}, f32[1,2048]{1,0:T(1,128)}, f32[1,6144]{1,0:T(1,128)}, bf16[2,32,6...) custom-call(bf16[2,16,6144]{2,1,0:T(8,128)(2,1)S(1)} %join.3.mine, ...), custom_call_target="tpu_custom_call", output_to_operand_aliasing={{9}: (5, {})} | custom-call | flops 4831838208 | bytes 75497472 | tf_op jit(solution)/shard_map/weights_pass/pallas_call | solution.py:157
  50.0 0.2 collective-permute-start.5
  50.2 2.5 %outer_rows.3 = (bf16[6144,2048]{1,0:T(8,128)(2,1)}, bf16[6144,2048]{1,0:T(8,128)(2,1)}, f32[8,128]{1,0:T(8,128)S(1)}) custom-call(bf16[2,32,6144]{2,1,0:T(8,128)(2,1)S(1)} %get-tuple-element.35.both, bf16[32,2048]{1,0:T(8,128)(2,1)S(1)} %get-tuple-element.36.active, ...), custom_call_target="tpu_custom_call", output_to_operand_aliasing={{0}: (3, {}), {1}: (4, {})} | custom-call | flops 134217728 | bytes 4194304 | tf_op jit(solution)/shard_map/outer_rows/pallas_call | solution.py:215
  52.7 0.1 add_and_split.2
  52.8 1.6 %collective-permute-start.6 = (bf16[2,8,6144]{2,1,0:T(8,128)(2,1)S(1)}, bf16[2,8,6144]{2,1,0:T(8,128)(2,1)S(1)}, u32[]{:S(2)}, u32[]{:S(2)}) collective-permute-start(bf16[2,8,6144]{2,1,0:T(8,128)(2,1)S(1)} %get-tuple-element.47), channel_id=1, source_target_pairs={{0,2},{1,3},{2,0},{3,1},{4,6},{5,7},{6,4},{7,5},{8,10},{9,11},{10,... | collective-permute-start | bytes 589832 | tf_op jit(solution)/shard_map/ppermute | solution.py:299
  54.4 6.7 %outer_rows.4 = (bf16[6144,2048]{1,0:T(8,128)(2,1)}, bf16[6144,2048]{1,0:T(8,128)(2,1)}, f32[8,128]{1,0:T(8,128)S(1)}) custom-call(bf16[2,32,6144]{2,1,0:T(8,128)(2,1)S(1)} %get-tuple-element.35.both, bf16[32,2048]{1,0:T(8,128)(2,1)S(1)} %get-tuple-element.36.active, ...), custom_call_target="tpu_custom_call", output_to_operand_aliasing={{0}: (3, {}), {1}: (4, {})} | custom-call | flops 536870912 | bytes 16777216 | tf_op jit(solution)/shard_map/outer_rows/pallas_call | solution.py:215
  61.1 0.1 add_and_split.3
  61.2 0.8 %collective-permute-start.7 = (bf16[2,2,6144]{2,1,0:T(2,128)(2,1)S(1)}, bf16[2,2,6144]{2,1,0:T(2,128)(2,1)S(1)}, u32[]{:S(2)}, u32[]{:S(2)}) collective-permute-start(bf16[2,2,6144]{2,1,0:T(2,128)(2,1)S(1)} %get-tuple-element.49), channel_id=1, source_target_pairs={{0,4},{1,5},{2,6},{3,7},{4,0},{5,1},{6,2},{7,3},{8,12},{9,13},{10,... | collective-permute-start | bytes 147464 | tf_op jit(solution)/shard_map/ppermute | solution.py:299
  62.0 1.9 %collective-permute-start.8 = (bf16[2,2,6144]{2,1,0:T(2,128)(2,1)S(1)}, bf16[2,2,6144]{2,1,0:T(2,128)(2,1)S(1)}, u32[]{:S(2)}, u32[]{:S(2)}) collective-permute-start(bf16[2,2,6144]{2,1,0:T(2,128)(2,1)S(1)} %get-tuple-element.50), channel_id=1, source_target_pairs={{0,8},{1,9},{2,10},{3,11},{4,12},{5,13},{6,14},{7,15},{8,0},{9,1},... | collective-permute-start | bytes 147464 | tf_op jit(solution)/shard_map/ppermute | solution.py:299
  63.9 1.8 %collective-permute-start.9 = (bf16[2,2,6144]{2,1,0:T(2,128)(2,1)S(1)}, bf16[2,2,6144]{2,1,0:T(2,128)(2,1)S(1)}, u32[]{:S(2)}, u32[]{:S(2)}) collective-permute-start(bf16[2,2,6144]{2,1,0:T(2,128)(2,1)S(1)} %get-tuple-element.51), channel_id=1, source_target_pairs={{0,12},{1,13},{2,14},{3,15},{4,8},{5,9},{6,10},{7,11},{8,4},{9,5},... | collective-permute-start | bytes 147464 | tf_op jit(solution)/shard_map/ppermute | solution.py:299
  65.7 5.5 %outer_rows.5 = (bf16[6144,2048]{1,0:T(8,128)(2,1)}, bf16[6144,2048]{1,0:T(8,128)(2,1)}, f32[8,128]{1,0:T(8,128)}) custom-call(bf16[2,32,6144]{2,1,0:T(8,128)(2,1)S(1)} %get-tuple-element.35.both, bf16[32,2048]{1,0:T(8,128)(2,1)S(1)} %get-tuple-element.36.active, ...), custom_call_target="tpu_custom_call", output_to_operand_aliasing={{0}: (3, {}), {1}: (4, {})} | custom-call | flops 402653184 | bytes 12582912 | tf_op jit(solution)/shard_map/outer_rows/pallas_call | solution.py:215
  71.2 0.7 last_sum.1
  (12 shorter events, 0.1 us)
Async XLA Ops:
  1.5 7.3 %collective-permute-start = (bf16[2,2,6144]{2,1,0:T(2,128)(2,1)S(1)}, bf16[2,2,6144]{2,1,0:T(2,128)(2,1)S(1)}, u32[]{:S(2)}, u32[]{:S(2)}) collective-permute-start(bf16[2,2,6144]{2,1,0:T(2,128)(2,1)S(1)} %pad_maximum_fusion.refs_3_), channel_id=1, source_target_pairs={{0,12},{1,13},{2,14},{3,15},{4,8},{5,9},{6,10},{7,11},{8,4},{9,5},... | collective-permute-start | bytes 147464 | tf_op jit(solution)/shard_map/ppermute | solution.py:299
  6.6 5.0 %collective-permute-start.1 = (bf16[2,2,6144]{2,1,0:T(2,128)(2,1)S(1)}, bf16[2,2,6144]{2,1,0:T(2,128)(2,1)S(1)}, u32[]{:S(2)}, u32[]{:S(2)}) collective-permute-start(bf16[2,2,6144]{2,1,0:T(2,128)(2,1)S(1)} %pad_maximum_fusion.refs_3_), channel_id=1, source_target_pairs={{0,8},{1,9},{2,10},{3,11},{4,12},{5,13},{6,14},{7,15},{8,0},{9,1},... | collective-permute-start | bytes 147464 | tf_op jit(solution)/shard_map/ppermute | solution.py:299
  6.6 5.0 %collective-permute-start.2 = (bf16[2,2,6144]{2,1,0:T(2,128)(2,1)S(1)}, bf16[2,2,6144]{2,1,0:T(2,128)(2,1)S(1)}, u32[]{:S(2)}, u32[]{:S(2)}) collective-permute-start(bf16[2,2,6144]{2,1,0:T(2,128)(2,1)S(1)} %pad_maximum_fusion.refs_3_), channel_id=1, source_target_pairs={{0,4},{1,5},{2,6},{3,7},{4,0},{5,1},{6,2},{7,3},{8,12},{9,13},{10,... | collective-permute-start | bytes 147464 | tf_op jit(solution)/shard_map/ppermute | solution.py:299
  11.7 5.8 %collective-permute-start.3 = (bf16[2,8,6144]{2,1,0:T(8,128)(2,1)S(1)}, bf16[2,8,6144]{2,1,0:T(8,128)(2,1)S(1)}, u32[]{:S(2)}, u32[]{:S(2)}) collective-permute-start(bf16[2,8,6144]{2,1,0:T(8,128)(2,1)S(1)} %join.2._mine.refs_1_), channel_id=1, source_target_pairs={{0,2},{1,3},{2,0},{3,1},{4,6},{5,7},{6,4},{7,5},{8,10},{9,11},{10,... | collective-permute-start | bytes 589832 | tf_op jit(solution)/shard_map/ppermute | solution.py:299
  17.5 1.8 %collective-permute-start.4 = (bf16[2,16,6144]{2,1,0:T(8,128)(2,1)S(1)}, bf16[2,16,6144]{2,1,0:T(8,128)(2,1)S(1)}, u32[]{:S(2)}, u32[]{:S(2)}) collective-permute-start(bf16[2,16,6144]{2,1,0:T(8,128)(2,1)S(1)} %join.3.mine), channel_id=1, source_target_pairs={{0,1},{1,0},{2,3},{3,2},{4,5},{5,4},{6,7},{7,6},{8,9},{9,8},{10,11... | collective-permute-start | bytes 1179656 | tf_op jit(solution)/shard_map/ppermute | solution.py:299
  50.0 2.7 %collective-permute-start.5 = (f32[2,16,6144]{2,1,0:T(8,128)S(1)}, f32[2,16,6144]{2,1,0:T(8,128)S(1)}, u32[]{:S(2)}, u32[]{:S(2)}) collective-permute-start(f32[2,16,6144]{2,1,0:T(8,128)S(1)} %get-tuple-element.45), channel_id=1, source_target_pairs={{0,1},{1,0},{2,3},{3,2},{4,5},{5,4},{6,7},{7,6},{8,9},{9,8},{10,11... | collective-permute-start | bytes 2359304 | tf_op jit(solution)/shard_map/ppermute | solution.py:299
  52.8 8.3 %collective-permute-start.6 = (bf16[2,8,6144]{2,1,0:T(8,128)(2,1)S(1)}, bf16[2,8,6144]{2,1,0:T(8,128)(2,1)S(1)}, u32[]{:S(2)}, u32[]{:S(2)}) collective-permute-start(bf16[2,8,6144]{2,1,0:T(8,128)(2,1)S(1)} %get-tuple-element.47), channel_id=1, source_target_pairs={{0,2},{1,3},{2,0},{3,1},{4,6},{5,7},{6,4},{7,5},{8,10},{9,11},{10,... | collective-permute-start | bytes 589832 | tf_op jit(solution)/shard_map/ppermute | solution.py:299
  54.4 11.3 %copy-start = (bf16[6144]{0:T(1024)(128)(2,1)S(1)}, bf16[6144]{0:T(1024)(128)(2,1)}, u32[]{:S(2)}) copy-start(bf16[6144]{0:T(1024)(128)(2,1)} %param.10) | copy-start | bytes 36868
  61.2 9.9 %collective-permute-start.7 = (bf16[2,2,6144]{2,1,0:T(2,128)(2,1)S(1)}, bf16[2,2,6144]{2,1,0:T(2,128)(2,1)S(1)}, u32[]{:S(2)}, u32[]{:S(2)}) collective-permute-start(bf16[2,2,6144]{2,1,0:T(2,128)(2,1)S(1)} %get-tuple-element.49), channel_id=1, source_target_pairs={{0,4},{1,5},{2,6},{3,7},{4,0},{5,1},{6,2},{7,3},{8,12},{9,13},{10,... | collective-permute-start | bytes 147464 | tf_op jit(solution)/shard_map/ppermute | solution.py:299
  62.0 9.2 %collective-permute-start.8 = (bf16[2,2,6144]{2,1,0:T(2,128)(2,1)S(1)}, bf16[2,2,6144]{2,1,0:T(2,128)(2,1)S(1)}, u32[]{:S(2)}, u32[]{:S(2)}) collective-permute-start(bf16[2,2,6144]{2,1,0:T(2,128)(2,1)S(1)} %get-tuple-element.50), channel_id=1, source_target_pairs={{0,8},{1,9},{2,10},{3,11},{4,12},{5,13},{6,14},{7,15},{8,0},{9,1},... | collective-permute-start | bytes 147464 | tf_op jit(solution)/shard_map/ppermute | solution.py:299
  63.9 7.3 %collective-permute-start.9 = (bf16[2,2,6144]{2,1,0:T(2,128)(2,1)S(1)}, bf16[2,2,6144]{2,1,0:T(2,128)(2,1)S(1)}, u32[]{:S(2)}, u32[]{:S(2)}) collective-permute-start(bf16[2,2,6144]{2,1,0:T(2,128)(2,1)S(1)} %get-tuple-element.51), channel_id=1, source_target_pairs={{0,12},{1,13},{2,14},{3,15},{4,8},{5,9},{6,10},{7,11},{8,4},{9,5},... | collective-permute-start | bytes 147464 | tf_op jit(solution)/shard_map/ppermute | solution.py:299
